TPU v7x, 512 devices: a whole 4x8x8 slice. The times are simulated.
512 devices in a mesh: ctx: 32 (over x, y), tp: 16 (over z, core).
Axes of the slice: x: 4, y: 8, z: 8, core: 2. Of those that a mesh axis runs over, the one named last changes fastest.
Arguments:
- tokens: bfloat16 [4096, 4096], P('ctx', 'tp'), may hold values from -6 to 6
- gate_values: bfloat16 [4096, 4096], P('ctx', 'tp'), may hold values from -6 to 6
- filters: bfloat16 [4096, 4096], P('ctx', 'tp'), may hold values from -1 to 1
- input_weight: bfloat16 [4096, 4096], P('ctx', 'tp'), may hold values from -0.09375 to 0.09375
- output_weight: bfloat16 [4096, 4096], P('tp', 'ctx'), may hold values from -0.09375 to 0.09375
- cotangent: bfloat16 [4096, 4096], P('ctx', 'tp'), may hold values from -6 to 6
Outputs:
- layer_output: bfloat16 [4096, 4096], P('ctx', 'tp')
- grad_tokens: bfloat16 [4096, 4096], P('ctx', 'tp')
- grad_gate: bfloat16 [4096, 4096], P('ctx', 'tp')
- grad_input_weight: bfloat16 [4096, 4096], P('ctx', 'tp')
- grad_output_weight: bfloat16 [4096, 4096], P('tp', 'ctx')
All inputs are finite; a program needn't handle non-finite values.
Results may differ from a plain program's by a relative error of at most 0.028.
Values may be sent and summed in bfloat16 or wider, within the bound.
No kernel may reach another device: no remote copies, remote signals or barrier semaphores. Data moves between devices by JAX's collectives and lax.ppermute only.
A program may use at most 64 MiB of HBM per device.

v0:
```python
import math

import jax
import jax.numpy as jnp
from jax import lax
from jax.sharding import PartitionSpec as P

exact_mode = lax.Precision.HIGHEST


def as_sent(x):

    def short(part):
        return part.astype(jnp.bfloat16) if part.dtype == jnp.float32 else part

    return jax.tree.map(short, x)


def angles(left_index, right_index, period):
    residue = left_index[:, None] * right_index[None, :] % period
    phases = residue.astype(jnp.float32) * (2.0 * math.pi / period)
    return (jnp.cos(phases), jnp.sin(phases))


def shaped(table):
    return table[:, :, None]


def rows_count(values):
    return values.shape[1]


def along_first(matrix, values):
    return jnp.einsum("kp,pxy->kxy", matrix, values, precision=exact_mode)


def along_rows(matrix, values):
    return jnp.einsum("kr,arc->akc", matrix, values, precision=exact_mode)


def time_to_mixed(blocks, row_index, block_freqs, fft_length):
    block_count = blocks.shape[0]
    cosine, sine_table = angles(
        jnp.arange(block_freqs, dtype=jnp.int32),
        jnp.arange(block_count, dtype=jnp.int32),
        block_freqs,
    )
    real_part = along_first(cosine, blocks)
    imag_part = -along_first(sine_table, blocks)
    twist_cos, twist_sin = angles(jnp.arange(block_freqs, dtype=jnp.int32), row_index, fft_length)
    twist_cos = shaped(twist_cos)
    twist_sin = shaped(twist_sin)
    return (
        real_part * twist_cos + imag_part * twist_sin,
        imag_part * twist_cos - real_part * twist_sin,
    )


def mixed_to_spectrum(real_part, imag_part):
    length = rows_count(real_part)
    steps_index = jnp.arange(length, dtype=jnp.int32)
    cosine, sine_table = angles(steps_index, steps_index, length)
    spec_real = along_rows(cosine, real_part) + along_rows(sine_table, imag_part)
    spec_imag = along_rows(cosine, imag_part) - along_rows(sine_table, real_part)
    return (spec_real, spec_imag)


def spectrum_to_mixed(real_part, imag_part, freq_index, fft_length):
    length = rows_count(real_part)
    steps_index = jnp.arange(length, dtype=jnp.int32)
    cosine, sine_table = angles(steps_index, steps_index, length)
    back_real = along_rows(cosine, real_part) - along_rows(sine_table, imag_part)
    back_imag = along_rows(cosine, imag_part) + along_rows(sine_table, real_part)
    twist_cos, twist_sin = angles(freq_index, steps_index, fft_length)
    twist_cos = shaped(twist_cos)
    twist_sin = shaped(twist_sin)
    return (
        back_real * twist_cos - back_imag * twist_sin,
        back_imag * twist_cos + back_real * twist_sin,
    )


def mixed_to_time(real_part, imag_part, block_count, fft_length):
    block_freqs = real_part.shape[0]
    cosine, sine_table = angles(
        jnp.arange(block_count, dtype=jnp.int32),
        jnp.arange(block_freqs, dtype=jnp.int32),
        block_freqs,
    )
    return (along_first(cosine, real_part) - along_first(sine_table, imag_part)) / fft_length


def apply_filter(spectrum, response, adjoint):
    if adjoint:
        return (
            spectrum[0] * response[0] + spectrum[1] * response[1],
            spectrum[1] * response[0] - spectrum[0] * response[1],
        )
    return (
        spectrum[0] * response[0] - spectrum[1] * response[1],
        spectrum[0] * response[1] + spectrum[1] * response[0],
    )


def on_device(tokens, gate_values, filters, input_weight, output_weight, cotangent):
    ctx_size = lax.axis_size("ctx")
    ctx_index = lax.axis_index("ctx")
    token_count = tokens.shape[0]
    channels = gate_values.shape[1]
    block_freqs = 2 * ctx_size
    fft_length = block_freqs * token_count
    all_features = lax.all_gather(tokens, "tp", axis=1, tiled=True)
    input_rows = lax.all_gather(input_weight, "ctx", axis=0, tiled=True)
    projected = jnp.dot(all_features, input_rows, preferred_element_type=jnp.float32).astype(
        jnp.bfloat16
    )

    def to_spectrum(values):
        blocks = lax.all_to_all(
            values.reshape(1, token_count, channels), "ctx", split_axis=1, concat_axis=0, tiled=True
        )
        per_device = blocks.shape[1]
        row_index = ctx_index * per_device + jnp.arange(per_device, dtype=jnp.int32)
        mixed_part = time_to_mixed(blocks.astype(jnp.float32), row_index, block_freqs, fft_length)
        regrouped = (
            lax.all_to_all(
                mixed_part[0].astype(jnp.bfloat16), "ctx", split_axis=0, concat_axis=1, tiled=True
            ).astype(jnp.float32),
            lax.all_to_all(
                mixed_part[1].astype(jnp.bfloat16), "ctx", split_axis=0, concat_axis=1, tiled=True
            ).astype(jnp.float32),
        )
        return mixed_to_spectrum(regrouped[0], regrouped[1])

    def from_spectrum(spectrum, response, adjoint):
        filtered = apply_filter(spectrum, response, adjoint)
        local_freqs = block_freqs // ctx_size
        freq_index = ctx_index * local_freqs + jnp.arange(local_freqs, dtype=jnp.int32)
        back_part = spectrum_to_mixed(filtered[0], filtered[1], freq_index, fft_length)
        joined = (
            lax.all_to_all(as_sent(back_part[0]), "ctx", split_axis=1, concat_axis=0, tiled=True),
            lax.all_to_all(as_sent(back_part[1]), "ctx", split_axis=1, concat_axis=0, tiled=True),
        )
        in_time = mixed_to_time(joined[0], joined[1], ctx_size, fft_length)
        returned = lax.all_to_all(
            as_sent(in_time), "ctx", split_axis=0, concat_axis=1, tiled=True
        ).astype(in_time.dtype)
        return returned.reshape(token_count, channels)

    response = to_spectrum(filters)
    convolved = from_spectrum(to_spectrum(projected), response, False)
    modulated = (gate_values.astype(jnp.float32) * convolved).astype(jnp.bfloat16)
    output_columns = lax.all_gather(output_weight, "ctx", axis=1, tiled=True)
    output_partial = jnp.dot(modulated, output_columns, preferred_element_type=jnp.float32)
    layer_output = lax.psum_scatter(
        output_partial.astype(jnp.bfloat16), "tp", scatter_dimension=1, tiled=True
    )
    cotangent_all = lax.all_gather(cotangent, "tp", axis=1, tiled=True)
    grad_modulated = lax.dot_general(
        cotangent_all, output_columns, (((1,), (1,)), ((), ())), preferred_element_type=jnp.float32
    )
    grad_gate = (grad_modulated * convolved).astype(jnp.bfloat16)
    grad_convolved = (grad_modulated * gate_values.astype(jnp.float32)).astype(jnp.bfloat16)
    grad_projected = from_spectrum(to_spectrum(grad_convolved), response, True).astype(jnp.bfloat16)
    input_partial = lax.dot_general(
        grad_projected, input_rows, (((1,), (1,)), ((), ())), preferred_element_type=jnp.float32
    )
    grad_tokens = lax.psum_scatter(
        input_partial.astype(jnp.bfloat16), "tp", scatter_dimension=1, tiled=True
    )
    weight_partial = lax.dot_general(
        all_features, grad_projected, (((0,), (0,)), ((), ())), preferred_element_type=jnp.float32
    )
    grad_input_weight = lax.psum_scatter(
        weight_partial.astype(jnp.bfloat16), "ctx", scatter_dimension=0, tiled=True
    )
    cotangent_cols = lax.all_to_all(cotangent_all, "ctx", split_axis=1, concat_axis=0, tiled=True)
    grad_output_weight = lax.dot_general(
        lax.all_gather(modulated, "ctx", axis=0, tiled=True),
        cotangent_cols,
        (((0,), (0,)), ((), ())),
        preferred_element_type=jnp.float32,
    ).astype(jnp.bfloat16)
    return (layer_output, grad_tokens, grad_gate, grad_input_weight, grad_output_weight)


def solution(mesh):
    placed = (
        P("ctx", "tp"),
        P("ctx", "tp"),
        P("ctx", "tp"),
        P("ctx", "tp"),
        P("tp", "ctx"),
        P("ctx", "tp"),
    )
    return jax.shard_map(
        on_device,
        mesh=mesh,
        in_specs=placed,
        out_specs=(P("ctx", "tp"), P("ctx", "tp"), P("ctx", "tp"), P("ctx", "tp"), P("tp", "ctx")),
        check_vma=False,
    )
```

profile of v0, /device:TPU:16, one launch (start us, length us, event | category | flops | bytes accessed | tf_op | source)
XLA Modules:
  0.0 863.2 jit_solution(10608363289715249459)
XLA Ops:
  7.2 0.7 all-gather.6.cloned.1.call-update
  7.9 0.7 all-gather.8.cloned.1.call-update
  8.7 1.6 copy.166
  10.9 0.9 copy.208
  12.3 1.0 reduce.7
  13.3 0.7 reshape.178
  14.0 10.0 %all-to-all-start.3 = ((bf16[32,2,512]{2,1,0:T(2,128)(2,1)}), bf16[32,2,512]{2,1,0:T(2,128)(2,1)S(1)}, u32[]{:S(2)}, u32[]{:S(2)}) async-start(bf16[32,2,512]{2,1,0:T(2,128)(2,1)} %reshape.178), calls=%async_computation.3 | async-start | bytes 131072 | tf_op jit(solution)/shard_map/all_to_all | solution.py:119
  24.2 8.2 all-to-all-done.3
  33.6 21.7 %all-gather.6.cloned.1.call-done = bf16[128,4096]{1,0:T(8,128)(2,1)} async-done(((bf16[128,256]{1,0:T(8,128)(2,1)}), bf16[128,4096]{1,0:T(8,128)(2,1)}) %all-gather.6.cloned.1.call-update) | async-done | bytes 1048592 | tf_op jit(solution)/shard_map/all_gather | solution.py:112
  55.4 84.8 %all-gather.8.cloned.1.call-done = bf16[4096,256]{1,0:T(8,128)(2,1)} async-done(((bf16[128,256]{1,0:T(8,128)(2,1)}), bf16[4096,256]{1,0:T(8,128)(2,1)}) %all-gather.8.cloned.1.call-update) | async-done | bytes 2097168 | tf_op jit(solution)/shard_map/all_gather | solution.py:113
  140.2 2.4 fusion.5
  142.7 1.0 reduce.8
  143.7 0.7 reshape.176
  144.4 6.5 all-to-all-start
  150.9 32.0 %all-gather.12.cloned.1.call-done = bf16[128,4096]{0,1:T(8,128)(2,1)} async-done(((bf16[128,256]{0,1:T(8,128)(2,1)}), bf16[128,4096]{0,1:T(8,128)(2,1)}) %all-gather.12.cloned.1.call-update) | async-done | bytes 1048592 | tf_op jit(solution)/shard_map/all_gather | solution.py:158
  182.9 80.5 %all-gather.10.cloned.1.call-done = bf16[256,4096]{1,0:T(8,128)(2,1)} async-done(((bf16[256,128]{1,0:T(8,128)(2,1)}), bf16[256,4096]{1,0:T(8,128)(2,1)}) %all-gather.10.cloned.1.call-update) | async-done | bytes 2097168 | tf_op jit(solution)/shard_map/all_gather | solution.py:153
  263.4 2.7 fusion.260
  266.2 1.0 reduce.6
  267.3 0.7 reshape.180
  267.9 8.7 %all-to-all-start.9 = ((bf16[32,2,512]{2,1,0:T(2,128)(2,1)}), bf16[32,2,512]{2,1,0:T(2,128)(2,1)S(1)}, u32[]{:S(2)}, u32[]{:S(2)}) async-start(bf16[32,2,512]{2,1,0:T(2,128)(2,1)} %reshape.180), calls=%async_computation.10 | async-start | bytes 131072 | tf_op jit(solution)/shard_map/all_to_all | solution.py:119
  277.9 7.1 all-to-all-done.9
  286.3 0.8 copy.154
  287.0 5.4 all-to-all-start.5
  292.5 0.8 copy.151
  293.2 8.3 all-to-all-done.5
  301.6 5.1 all-to-all-start.4
  306.7 0.8 copy.170
  307.4 8.3 all-to-all-done.4
  315.7 5.1 all-to-all-start.10
  320.9 0.8 copy.173
  321.7 0.8 copy.145
  322.4 0.8 copy.142
  324.2 5.6 all-to-all-done.10
  329.9 5.1 all-to-all-start.11
  336.8 7.2 all-to-all-done.11
  344.0 5.1 all-to-all-start.2
  350.5 7.8 all-to-all-done.2
  358.2 5.1 all-to-all-start.1
  364.6 7.8 all-to-all-done.1
  379.2 0.7 fusion.23
  379.9 0.8 copy.161
  380.7 5.3 all-to-all-start.6
  386.0 0.8 copy.163
  386.8 9.5 %all-to-all-done.6 = bf16[2,128,256]{2,0,1:T(2,128)(2,1)S(1)} async-done(((bf16[2,128,256]{2,0,1:T(2,128)(2,1)}), bf16[2,128,256]{2,0,1:T(2,128)(2,1)S(1)}, u32[]{:S(2)}, u32[]{:S(2)}) %all-to-all-start.6) | async-done | bytes 131104 | tf_op jit(solution)/shard_map/all_to_all | solution.py:141
  396.2 5.1 all-to-all-start.7
  401.9 8.4 all-to-all-done.7
  410.8 13.3 %all_to_all.256 = bf16[32,4,256]{2,1,0:T(4,128)(2,1)S(1)} all-to-all(bf16[32,4,256]{2,1,0:T(4,128)(2,1)S(1)} %copy.165), channel_id=1, replica_groups=mesh['ctx'=32,'tp'=16] {'ctx'}, dimensions={0} | all-to-all | bytes 131072 | tf_op jit(solution)/shard_map/all_to_all | solution.py:145
  424.9 2.3 convolution_convert_fusion.2
  427.2 0.8 copy.178
  428.0 5.4 all-to-all-start.12
  433.5 0.8 copy.180
  434.3 8.3 all-to-all-done.12
  442.6 5.1 all-to-all-start.13
  447.9 9.0 %all-to-all-done.13 = bf16[2,128,256]{2,0,1:T(2,128)(2,1)S(1)} async-done(((bf16[2,128,256]{2,0,1:T(2,128)(2,1)}), bf16[2,128,256]{2,0,1:T(2,128)(2,1)S(1)}, u32[]{:S(2)}, u32[]{:S(2)}) %all-to-all-start.13) | async-done | bytes 131104 | tf_op jit(solution)/shard_map/all_to_all | solution.py:142
  457.7 15.2 %all_to_all.257 = bf16[32,4,256]{2,1,0:T(4,128)(2,1)S(1)} all-to-all(bf16[32,4,256]{2,1,0:T(4,128)(2,1)S(1)} %copy.182), channel_id=1, replica_groups=mesh['ctx'=32,'tp'=16] {'ctx'}, dimensions={0} | all-to-all | bytes 131072 | tf_op jit(solution)/shard_map/all_to_all | solution.py:145
  472.9 1.8 convolution_convert_fusion.1
  474.7 0.7 fusion
  475.5 2.5 copy.185
  478.0 1.2 copy-done.3
  479.2 27.4 %all_to_all.258 = bf16[128,32,128]{0,2,1:T(8,128)(2,1)S(1)} all-to-all(bf16[128,32,128]{0,2,1:T(8,128)(2,1)S(1)} %bitcast.200), channel_id=1, replica_groups=mesh['ctx'=32,'tp'=16] {'ctx'}, dimensions={1} | all-to-all | bytes 2097152 | tf_op jit(solution)/shard_map/all_to_all | solution.py:177
  507.3 3.0 convolution_convert_fusion.3
  510.3 59.6 %reduce-scatter.6.cloned.1.call-done = bf16[128,256]{1,0:T(8,128)(2,1)} async-done(((bf16[128,4096]{1,0:T(8,128)(2,1)}), bf16[128,256]{1,0:T(8,128)(2,1)}) %reduce-scatter.6.cloned.1.call-update) | async-done | bytes 65552 | tf_op jit(solution)/shard_map/reduce_scatter | solution.py:155
  569.9 62.2 %reduce-scatter.8.cloned.1.call-done = bf16[128,256]{1,0:T(8,128)(2,1)} async-done(((bf16[128,4096]{1,0:T(8,128)(2,1)}), bf16[128,256]{1,0:T(8,128)(2,1)}) %reduce-scatter.8.cloned.1.call-update) | async-done | bytes 65552 | tf_op jit(solution)/shard_map/reduce_scatter | solution.py:168
  632.1 224.3 %reduce-scatter.10.cloned.1.call-done = bf16[128,256]{1,0:T(8,128)(2,1)} async-done(((bf16[4096,256]{1,0:T(8,128)(2,1)}), bf16[128,256]{1,0:T(8,128)(2,1)}) %reduce-scatter.10.cloned.1.call-update) | async-done | bytes 65552
  (97 shorter events, 20.9 us)
Async XLA Ops:
  7.2 48.2 %all-gather.6.cloned.1.call-start = ((), (), s32[]{:S(2)}) async-start(), calls=%async_computation.19 | async-start | bytes 1114112 | tf_op jit(solution)/shard_map/all_gather | solution.py:112
  7.9 132.3 %all-gather.8.cloned.1.call-start = ((), (), s32[]{:S(2)}) async-start(), calls=%async_computation.20 | async-start | bytes 2162688 | tf_op jit(solution)/shard_map/all_gather | solution.py:113
  8.6 174.2 %all-gather.12.cloned.1.call-start = ((), (), s32[]{:S(2)}) async-start(), calls=%async_computation.23 | async-start | bytes 1114112 | tf_op jit(solution)/shard_map/all_gather | solution.py:158
  10.3 253.1 %all-gather.10.cloned.1.call-start = ((), (), s32[]{:S(2)}) async-start(), calls=%async_computation.21 | async-start | bytes 2162688 | tf_op jit(solution)/shard_map/all_gather | solution.py:153
  14.0 18.4 %all-to-all-start.3 = ((bf16[32,2,512]{2,1,0:T(2,128)(2,1)}), bf16[32,2,512]{2,1,0:T(2,128)(2,1)S(1)}, u32[]{:S(2)}, u32[]{:S(2)}) async-start(bf16[32,2,512]{2,1,0:T(2,128)(2,1)} %reshape.178), calls=%async_computation.3 | async-start | bytes 131072 | tf_op jit(solution)/shard_map/all_to_all | solution.py:119
  142.6 123.5 %copy-start.4 = (bf16[128,256]{1,0:T(8,128)(2,1)S(1)}, bf16[128,256]{1,0:T(8,128)(2,1)}, u32[]{:S(2)}) copy-start(bf16[128,256]{1,0:T(8,128)(2,1)} %param.7) | copy-start | bytes 196612
  144.4 123.5 %all-to-all-start = ((bf16[32,2,512]{2,1,0:T(2,128)(2,1)}), bf16[32,2,512]{2,1,0:T(2,128)(2,1)S(1)}, u32[]{:S(2)}, u32[]{:S(2)}) async-start(bf16[32,2,512]{2,1,0:T(2,128)(2,1)} %reshape.176), calls=%async_computation | async-start | bytes 131072 | tf_op jit(solution)/shard_map/all_to_all | solution.py:119
  267.9 17.0 %all-to-all-start.9 = ((bf16[32,2,512]{2,1,0:T(2,128)(2,1)}), bf16[32,2,512]{2,1,0:T(2,128)(2,1)S(1)}, u32[]{:S(2)}, u32[]{:S(2)}) async-start(bf16[32,2,512]{2,1,0:T(2,128)(2,1)} %reshape.180), calls=%async_computation.10 | async-start | bytes 131072 | tf_op jit(solution)/shard_map/all_to_all | solution.py:119
  287.0 14.5 %all-to-all-start.5 = ((bf16[64,4,256]{2,1,0:T(4,128)(2,1)}), bf16[64,4,256]{2,1,0:T(4,128)(2,1)S(1)}, u32[]{:S(2)}, u32[]{:S(2)}) async-start(bf16[64,4,256]{2,1,0:T(4,128)(2,1)} %copy.154), calls=%async_computation.5 | async-start | bytes 262144 | tf_op jit(solution)/shard_map/all_to_all | solution.py:129
  301.6 14.1 %all-to-all-start.4 = ((bf16[64,4,256]{2,1,0:T(4,128)(2,1)}), bf16[64,4,256]{2,1,0:T(4,128)(2,1)S(1)}, u32[]{:S(2)}, u32[]{:S(2)}) async-start(bf16[64,4,256]{2,1,0:T(4,128)(2,1)} %copy.151), calls=%async_computation.4 | async-start | bytes 262144 | tf_op jit(solution)/shard_map/all_to_all | solution.py:126
  315.7 14.1 %all-to-all-start.10 = ((bf16[64,4,256]{2,1,0:T(4,128)(2,1)}), bf16[64,4,256]{2,1,0:T(4,128)(2,1)S(1)}, u32[]{:S(2)}, u32[]{:S(2)}) async-start(bf16[64,4,256]{2,1,0:T(4,128)(2,1)} %copy.170), calls=%async_computation.11 | async-start | bytes 262144 | tf_op jit(solution)/shard_map/all_to_all | solution.py:126
  329.9 14.2 %all-to-all-start.11 = ((bf16[64,4,256]{2,1,0:T(4,128)(2,1)}), bf16[64,4,256]{2,1,0:T(4,128)(2,1)S(1)}, u32[]{:S(2)}, u32[]{:S(2)}) async-start(bf16[64,4,256]{2,1,0:T(4,128)(2,1)} %copy.173), calls=%async_computation.12 | async-start | bytes 262144 | tf_op jit(solution)/shard_map/all_to_all | solution.py:129
  344.0 14.2 %all-to-all-start.2 = ((bf16[64,4,256]{2,1,0:T(4,128)(2,1)}), bf16[64,4,256]{2,1,0:T(4,128)(2,1)S(1)}, u32[]{:S(2)}, u32[]{:S(2)}) async-start(bf16[64,4,256]{2,1,0:T(4,128)(2,1)} %copy.145), calls=%async_computation.2 | async-start | bytes 262144 | tf_op jit(solution)/shard_map/all_to_all | solution.py:129
  358.2 14.1 %all-to-all-start.1 = ((bf16[64,4,256]{2,1,0:T(4,128)(2,1)}), bf16[64,4,256]{2,1,0:T(4,128)(2,1)S(1)}, u32[]{:S(2)}, u32[]{:S(2)}) async-start(bf16[64,4,256]{2,1,0:T(4,128)(2,1)} %copy.142), calls=%async_computation.1 | async-start | bytes 262144 | tf_op jit(solution)/shard_map/all_to_all | solution.py:126
  379.9 45.0 %copy-start.1 = (bf16[256,4096]{1,0:T(8,128)(2,1)S(1)}, bf16[256,4096]{1,0:T(8,128)(2,1)}, u32[]{:S(2)}) copy-start(bf16[256,4096]{1,0:T(8,128)(2,1)} %all-gather.10.cloned.1.call-done) | copy-start | bytes 6291460
  380.7 15.5 %all-to-all-start.6 = ((bf16[2,128,256]{2,0,1:T(2,128)(2,1)}), bf16[2,128,256]{2,0,1:T(2,128)(2,1)S(1)}, u32[]{:S(2)}, u32[]{:S(2)}) async-start(bf16[2,128,256]{2,0,1:T(2,128)(2,1)} %copy.161), calls=%async_computation.6 | async-start | bytes 262144 | tf_op jit(solution)/shard_map/all_to_all | solution.py:141
  396.2 14.0 %all-to-all-start.7 = ((bf16[2,128,256]{2,0,1:T(2,128)(2,1)}), bf16[2,128,256]{2,0,1:T(2,128)(2,1)S(1)}, u32[]{:S(2)}, u32[]{:S(2)}) async-start(bf16[2,128,256]{2,0,1:T(2,128)(2,1)} %copy.163), calls=%async_computation.7 | async-start | bytes 262144 | tf_op jit(solution)/shard_map/all_to_all | solution.py:142
  401.4 105.9 %all-gather.14.cloned.1.call-start = ((), (), s32[]{:S(2)}) async-start(), calls=%async_computation.25 | async-start | bytes 2162688 | tf_op jit(solution)/shard_map/all_gather | solution.py:179
  424.8 145.0 %reduce-scatter.6.cloned.1.call-start = ((), (), s32[]{:S(2)}) async-start(), calls=%async_computation.22 | async-start | bytes 1114112 | tf_op jit(solution)/shard_map/reduce_scatter | solution.py:155
  427.2 45.7 %copy-start = (bf16[4096,256]{1,0:T(8,128)(2,1)S(1)}, bf16[4096,256]{1,0:T(8,128)(2,1)}, u32[]{:S(2)}) copy-start(bf16[4096,256]{1,0:T(8,128)(2,1)} %all-gather.8.cloned.1.call-done) | copy-start | bytes 6291460
  428.0 14.5 %all-to-all-start.12 = ((bf16[2,128,256]{2,0,1:T(2,128)(2,1)}), bf16[2,128,256]{2,0,1:T(2,128)(2,1)S(1)}, u32[]{:S(2)}, u32[]{:S(2)}) async-start(bf16[2,128,256]{2,0,1:T(2,128)(2,1)} %copy.178), calls=%async_computation.13 | async-start | bytes 262144 | tf_op jit(solution)/shard_map/all_to_all | solution.py:141
  442.6 14.3 %all-to-all-start.13 = ((bf16[2,128,256]{2,0,1:T(2,128)(2,1)}), bf16[2,128,256]{2,0,1:T(2,128)(2,1)S(1)}, u32[]{:S(2)}, u32[]{:S(2)}) async-start(bf16[2,128,256]{2,0,1:T(2,128)(2,1)} %copy.180), calls=%async_computation.14 | async-start | bytes 262144 | tf_op jit(solution)/shard_map/all_to_all | solution.py:142
  447.7 184.4 %reduce-scatter.8.cloned.1.call-start = ((), (), s32[]{:S(2)}) async-start(), calls=%async_computation.24 | async-start | bytes 1114112 | tf_op jit(solution)/shard_map/reduce_scatter | solution.py:168
  472.9 1.9 copy-start.2
  474.7 381.7 %reduce-scatter.10.cloned.1.call-start = ((), (), s32[]{:S(2)}) async-start(), calls=%async_computation.26 | async-start | bytes 2162688
  478.0 1.2 copy-start.3
Sparse Core Ops, SparseCore 0:
  10.0 45.2 all-gather.5
  58.5 81.6 all-gather.7
  142.9 39.9 all-gather.11
  185.8 77.5 all-gather.9
  425.0 81.9 all-gather.13
  510.2 59.6 reduce-scatter.5
  573.5 58.5 reduce-scatter.7
  637.1 219.2 reduce-scatter.9
where the time goes:
time: 865 us; the launch traced here: 863 us
  waiting for transfers between devices  663 us (77%)
  starting transfers between devices  77.3 us (9%)
  blocking collectives  56 us (6%)
  matrix products  27.8 us (3%)
  local copies, waits for them, and re-layouts  20.8 us (2%)
  between operations  14.8 us (2%)
    unnamed x9, waiting for transfers between devices  226 us
    all_gather x1, waiting for transfers between devices, on_device(): input_rows = lax.all_gather(input_weight, 'ctx', axis=0, tiled=True)  84.8 us
    all_gather x1, waiting for transfers between devices, on_device(): output_columns = lax.all_gather(output_weight, 'ctx', axis=1, tiled=True)  80.5 us
    reduce_scatter x1, waiting for transfers between devices, on_device(): lax.psum_scatter(input_partial.astype(jnp.bfloat16), 'tp', scatter_dimens...  62.2 us
    reduce_scatter x1, waiting for transfers between devices, on_device(): lax.psum_scatter(output_partial.astype(jnp.bfloat16), 'tp', scatter_dimen...  59.6 us
    all_gather x1, waiting for transfers between devices, on_device(): cotangent_all = lax.all_gather(cotangent, 'tp', axis=1, tiled=True)  32 us
    all_to_all x2, blocking collectives, from_spectrum(): lax.all_to_all(as_sent(in_time), 'ctx', split_axis=0, concat_axis=1, tile...  28.5 us
    all_to_all x1, blocking collectives, on_device(): lax.all_to_all(cotangent_all, 'ctx', split_axis=1, concat_axis=0, tiled=T...  27.4 us
  transfers between devices with their start and end apart: 21, of which 19 were waited for; matrix products, arithmetic and copies ran while one was open for 5% of the time, Pallas kernels for 0%

commit v1 on v0

v1 whole, which is shorter than its diff:
```python
import math

import jax
import jax.numpy as jnp
import numpy as np
from jax import lax
from jax.experimental import pallas as pl
from jax.experimental.pallas import tpu as pltpu
from jax.sharding import Mesh, PartitionSpec as P

bf16 = jnp.bfloat16
f32 = jnp.float32

NX, NY, NH, NL, NC = 4, 8, 4, 2, 2
CTX = ("x", "y")
TP = ("zh", "zl", "core")
ALL = CTX + TP
Z = ("zh", "zl")

BLOCKS = NX * NY
ROWS = 128
FREQS = 2 * BLOCKS
LENGTH = FREQS * ROWS
OWN = 8

VMEM = pl.BlockSpec(memory_space=pltpu.VMEM)
SMEM = pl.BlockSpec(memory_space=pltpu.SMEM)
PARAMS = pltpu.CompilerParams(vmem_limit_bytes=48 * 1024 * 1024)


def swap_pairs():
    def place(x, y, h, l, c):
        return (((x * NY + y) * NH + h) * NL + l) * NC + c

    return [
        (place(x, y, h, l, c), place(h, y, x, l, c))
        for x in range(NX)
        for y in range(NY)
        for h in range(NH)
        for l in range(NL)
        for c in range(NC)
    ]


def tables():
    freq = np.arange(FREQS)
    block = np.arange(BLOCKS)
    row = np.arange(ROWS)
    angle = 2 * math.pi * (freq[:, None] * block[None, :] % FREQS) / FREQS
    first = np.concatenate([np.cos(angle), -np.sin(angle)], 0)
    twist = 2 * math.pi * (freq[:, None] * row[None, :] % LENGTH) / LENGTH
    angle = 2 * math.pi * (row[:, None] * row[None, :] % ROWS) / ROWS
    cosine, sine = np.cos(angle), np.sin(angle)
    second = np.block([[cosine, -sine], [sine, cosine]])
    return (
        jnp.asarray(first, bf16),
        jnp.asarray(first.T, bf16),
        jnp.asarray(np.cos(twist), f32),
        jnp.asarray(np.sin(twist), f32),
        jnp.asarray(second, bf16),
        jnp.asarray(second.T, bf16),
    )


def dot(left, right):
    return jnp.dot(left, right, preferred_element_type=f32)


def weight_block(weights, which, l, c):
    first = 4 * l + 2 * c
    return jnp.concatenate([weights[first, which], weights[first + 1, which]], 0)


def project_kernel(me_ref, own, other, weights, filters, gate, out):
    me = me_ref[0]
    for which in range(2):
        total = None
        for l in range(NL):
            for held, c in ((own, me), (other, 1 - me)):
                rows = held[:, l, which].reshape(NX * ROWS, 2 * ROWS)
                term = dot(rows, weight_block(weights, which, l, c))
                total = term if total is None else total + term
        out[:, which * NX * ROWS : (which + 1) * NX * ROWS] = total.T.astype(bf16)
    base = 2 * NX * ROWS
    out[:, base : base + ROWS] = filters[...].astype(f32).T.astype(bf16)
    out[:, base + ROWS : base + 2 * ROWS] = gate[...].astype(f32).T.astype(bf16)


def convolve_kernel(
    got, first, first_back, twist_cos, twist_sin, second, second_back, out,
    proj, gmod, filt, gate, mixed, spectrum, product, back, o_mod, o_gp, o_gg,
):
    half = NX * ROWS

    def lanes(start):
        return slice(start, start + ROWS)

    for y in range(NY):
        for x in range(NX):
            b = x * NY + y
            at = slice(b * OWN, (b + 1) * OWN)
            for base, held in ((0, proj), (half, gmod)):
                total = got[y, :, lanes(base + x * ROWS)].astype(f32)
                for k in range(1, NX):
                    total = total + got[k * NY + y, :, lanes(base + x * ROWS)].astype(f32)
                held[at, :] = total
            filt[at, :] = got[b, :, lanes(2 * half)].astype(f32)
            gate[at, :] = got[b, :, lanes(2 * half + ROWS)].astype(f32)
    cosine, sine = twist_cos[...], twist_sin[...]
    for c in range(OWN):
        pick = pl.ds(c, BLOCKS, stride=OWN)
        signals = jnp.concatenate(
            [
                proj[pick, :].astype(bf16),
                (gmod[pick, :] * gate[pick, :]).astype(bf16),
                filt[pick, :].astype(bf16),
            ],
            1,
        )
        parts = dot(first[...], signals)
        for i in range(3):
            real = parts[:FREQS, lanes(i * ROWS)]
            imag = parts[FREQS:, lanes(i * ROWS)]
            at = slice((c * 3 + i) * FREQS, (c * 3 + i + 1) * FREQS)
            mixed[at, :ROWS] = (real * cosine + imag * sine).astype(bf16)
            mixed[at, ROWS:] = (imag * cosine - real * sine).astype(bf16)
    spectrum[...] = dot(mixed[...], second[...])
    for c in range(OWN):
        (xr, xi), (gr, gi), (hr, hi) = [
            (spectrum[at, :ROWS], spectrum[at, ROWS:])
            for at in [slice((c * 3 + i) * FREQS, (c * 3 + i + 1) * FREQS) for i in range(3)]
        ]
        at = slice(2 * c * FREQS, (2 * c + 1) * FREQS)
        product[at, :ROWS] = (xr * hr - xi * hi).astype(bf16)
        product[at, ROWS:] = (xr * hi + xi * hr).astype(bf16)
        at = slice((2 * c + 1) * FREQS, (2 * c + 2) * FREQS)
        product[at, :ROWS] = (gr * hr + gi * hi).astype(bf16)
        product[at, ROWS:] = (gi * hr - gr * hi).astype(bf16)
    back[...] = dot(product[...], second_back[...])
    for c in range(OWN):
        pick = pl.ds(c, BLOCKS, stride=OWN)
        columns = []
        for i in range(2):
            at = slice((2 * c + i) * FREQS, (2 * c + i + 1) * FREQS)
            real, imag = back[at, :ROWS], back[at, ROWS:]
            columns.append(
                jnp.concatenate(
                    [
                        (real * cosine - imag * sine).astype(bf16),
                        (imag * cosine + real * sine).astype(bf16),
                    ],
                    0,
                )
            )
        in_time = dot(first_back[...], jnp.concatenate(columns, 1)) * (1.0 / LENGTH)
        convolved = in_time[:, :ROWS]
        o_gp[pick, :] = in_time[:, ROWS:]
        o_mod[pick, :] = gate[pick, :] * convolved
        o_gg[pick, :] = gmod[pick, :] * convolved
    for y in range(NY):
        for x in range(NX):
            b = x * NY + y
            at = slice(b * OWN, (b + 1) * OWN)
            modulated = o_mod[at, :].astype(bf16)
            grad = o_gp[at, :].astype(bf16)
            for k in range(NX):
                out[k * NY + y, :, lanes(x * ROWS)] = modulated
                out[k * NY + y, :, lanes(half + x * ROWS)] = grad
            out[b, :, lanes(2 * half)] = o_gg[at, :].astype(bf16)


def weight_grad_kernel(me_ref, got, own, other, out):
    me = me_ref[0]
    half = NX * ROWS
    for which in range(2):
        left = got[:, half:] if which == 0 else got[:, :half]
        for l in range(NL):
            for held, c in ((own, me), (other, 1 - me)):
                rows = held[:, l, which].reshape(half, 2 * ROWS)
                total = dot(left, rows).astype(bf16)
                out[4 * l + 2 * c, which] = total[:, :ROWS]
                out[4 * l + 2 * c + 1, which] = total[:, ROWS:]


def output_kernel(me_ref, got, weights, keep, send):
    me = me_ref[0]
    half = NX * ROWS
    for which in range(2):
        start = which * half
        rows = got[:, start : start + half].astype(f32).T.astype(bf16)
        for l in range(NL):
            for held, c in ((keep, me), (send, 1 - me)):
                block = weight_block(weights, 1 - which, l, c)
                total = lax.dot_general(
                    rows, block, (((1,), (1,)), ((), ())), preferred_element_type=f32
                )
                held[:, l, which] = total.astype(bf16).reshape(NX, ROWS, 2 * ROWS)


def call(kernel, inputs, out_shape, flops, scratch=(), first_smem=True):
    specs = [VMEM] * len(inputs)
    if first_smem:
        specs[0] = SMEM
    many = isinstance(out_shape, tuple)
    return pl.pallas_call(
        kernel,
        out_shape=out_shape,
        in_specs=specs,
        out_specs=(VMEM,) * len(out_shape) if many else VMEM,
        scratch_shapes=list(scratch),
        compiler_params=PARAMS,
        cost_estimate=pl.CostEstimate(
            flops=flops,
            bytes_accessed=sum(a.size * a.dtype.itemsize for a in inputs),
            transcendentals=0,
        ),
    )(*inputs)


def on_device(tokens, gate_values, filters, input_weight, output_weight, cotangent):
    tokens_here, features = tokens.shape
    channels = gate_values.shape[1]
    me = lax.axis_index("core").astype(jnp.int32).reshape(1)
    swap = swap_pairs()

    weights = lax.all_gather(jnp.stack([input_weight, output_weight.T]), "y", axis=0)
    moved = jnp.stack([lax.ppermute(tokens, ALL, swap), lax.ppermute(cotangent, ALL, swap)])
    copies = jnp.broadcast_to(moved[None], (NH * NL, 2, tokens_here, features))
    own = lax.all_to_all(copies, Z, split_axis=0, concat_axis=0, tiled=True)
    other = lax.ppermute(own, "core", [(0, 1), (1, 0)])
    held = (NH, NL, 2, tokens_here, features)
    own, other = own.reshape(held), other.reshape(held)

    half = NX * ROWS
    sent = call(
        project_kernel,
        (me, own, other, weights, filters, gate_values),
        jax.ShapeDtypeStruct((channels, 2 * half + 2 * ROWS), bf16),
        4 * half * 1024 * channels,
    )
    got = lax.all_to_all(
        sent.reshape(BLOCKS, OWN, 2 * half + 2 * ROWS), CTX, split_axis=0, concat_axis=0, tiled=True
    )
    per_channel = pltpu.VMEM((BLOCKS * OWN, ROWS), f32)
    sent = call(
        convolve_kernel,
        (got,) + tables(),
        jax.ShapeDtypeStruct((BLOCKS, OWN, 2 * half + ROWS), bf16),
        2 * 40 * OWN * FREQS * 256 * 256,
        [per_channel] * 4
        + [
            pltpu.VMEM((3 * OWN * FREQS, 2 * ROWS), bf16),
            pltpu.VMEM((3 * OWN * FREQS, 2 * ROWS), f32),
            pltpu.VMEM((2 * OWN * FREQS, 2 * ROWS), bf16),
            pltpu.VMEM((2 * OWN * FREQS, 2 * ROWS), f32),
        ]
        + [per_channel] * 3,
        first_smem=False,
    )
    got = lax.all_to_all(sent, CTX, split_axis=0, concat_axis=0, tiled=True)
    got = got.reshape(channels, 2 * half + ROWS)
    streams, grad_gate = got[:, : 2 * half], got[:, 2 * half :].T

    grads = call(
        weight_grad_kernel,
        (me, streams, own, other),
        jax.ShapeDtypeStruct((NY, 2, channels, ROWS), bf16),
        4 * half * 1024 * channels,
    )
    grads = lax.psum_scatter(grads, "y", scatter_dimension=0, tiled=True)
    grad_input_weight, grad_output_weight = grads[0, 0].T, grads[0, 1]

    shape = jax.ShapeDtypeStruct(held, bf16)
    keep, send = call(
        output_kernel, (me, streams, weights), (shape, shape), 4 * half * 1024 * channels
    )
    arrived = lax.ppermute(send, "core", [(0, 1), (1, 0)])
    parts = (keep.astype(f32) + arrived.astype(f32)).astype(bf16)
    parts = lax.all_to_all(
        parts.reshape(NH * NL, 2, tokens_here, features), Z, split_axis=0, concat_axis=0, tiled=True
    )
    total = jnp.sum(parts.astype(f32), 0).astype(bf16)
    layer_output = lax.ppermute(total[0], ALL, swap)
    grad_tokens = lax.ppermute(total[1], ALL, swap)
    return (layer_output, grad_tokens, grad_gate, grad_input_weight, grad_output_weight)


def solution(mesh):
    chips = Mesh(mesh.devices.reshape(NX, NY, NH, NL, NC), ALL)
    rows, columns = P(CTX, TP), P(TP, CTX)
    return jax.shard_map(
        on_device,
        mesh=chips,
        in_specs=(rows, rows, rows, rows, columns, rows),
        out_specs=(rows, rows, rows, rows, columns),
        check_vma=False,
    )
```

time: 865 us -> 199 us (0.23)
  the two profiles are of different devices: /device:TPU:16 before, /device:TPU:4 now
where the time goes in v1:
time: 199 us; the launch traced here: 198 us
  waiting for transfers between devices  86.3 us (43%)
  blocking collectives  40.9 us (21%)
  starting transfers between devices  40.1 us (20%)
  between operations  14.3 us (7%)
  local copies, waits for them, and re-layouts  7.62 us (4%)
  Pallas kernels  5.62 us (3%)
  other arithmetic  3.35 us (2%)
    all_to_all x1, waiting for transfers between devices, on_device(): lax.all_to_all(parts.reshape(NH * NL, 2, tokens_here, features), Z, split...  27.5 us
    all_to_all x1, waiting for transfers between devices, on_device(): own = lax.all_to_all(copies, Z, split_axis=0, concat_axis=0, tiled=True)  26.6 us
    all_to_all x1, blocking collectives, on_device(): lax.all_to_all(sent.reshape(BLOCKS, OWN, 2 * half + 2 * ROWS), CTX, split...  20.8 us
    all_to_all x1, blocking collectives, on_device(): got = lax.all_to_all(sent, CTX, split_axis=0, concat_axis=0, tiled=True)  20.1 us
    all_gather x1, waiting for transfers between devices, on_device(): lax.all_gather(jnp.stack([input_weight, output_weight.T]), 'y', axis=0)  17.5 us
    ppermute x1, starting transfers between devices, on_device(): lax.ppermute(tokens, ALL, swap)  10.9 us
    ppermute x1, waiting for transfers between devices, on_device(): lax.ppermute(cotangent, ALL, swap)  9.67 us
    all_to_all x1, starting transfers between devices, on_device(): lax.all_to_all(parts.reshape(NH * NL, 2, tokens_here, features), Z, split...  7.55 us
  transfers between devices with their start and end apart: 10, of which 7 were waited for; matrix products, arithmetic and copies ran while one was open for 4% of the time, Pallas kernels for 1%

profile of v1, /device:TPU:4, one launch (start us, length us, event | category | flops | bytes accessed | tf_op | source)
XLA Modules:
  0.0 198.1 jit_solution(2953155527787713011)
XLA Ops:
  7.2 10.9 %collective-permute-start = (bf16[128,256]{1,0:T(8,128)(2,1)}, bf16[128,256]{1,0:T(8,128)(2,1)S(1)}, u32[]{:S(2)}, u32[]{:S(2)}) collective-permute-start(bf16[128,256]{1,0:T(8,128)(2,1)} %param.12), channel_id=1, source_target_pairs={{0,0},{1,1},{2,2},{3,3},{4,128},{5,129},{6,130},{7,131},{8,256},{9... | collective-permute-start | bytes 196616 | tf_op jit(solution)/shard_map/ppermute | solution.py:227
  18.0 1.9 collective-permute-start.1
  20.0 1.1 collective-permute-done
  21.0 9.7 %collective-permute-done.1 = bf16[128,256]{1,0:T(8,128)(2,1)S(1)} collective-permute-done((bf16[128,256]{1,0:T(8,128)(2,1)}, bf16[128,256]{1,0:T(8,128)(2,1)S(1)}, u32[]{:S(2)}, u32[]{:S(2)}) %collective-permute-start.1) | collective-permute-done | bytes 65568 | tf_op jit(solution)/shard_map/ppermute | solution.py:227
  30.7 1.1 broadcast_in_dim.2
  31.8 0.0 copy-start.11
  31.8 0.0 copy-start.2
  31.8 0.0 copy-start.3
  31.8 3.7 %all-to-all-start = ((bf16[8,2,128,256]{3,2,1,0:T(8,128)(2,1)}), bf16[8,2,128,256]{3,2,1,0:T(8,128)(2,1)S(1)}, u32[]{:S(2)}, u32[]{:S(2)}) async-start(bf16[8,2,128,256]{3,2,1,0:T(8,128)(2,1)} %broadcast_in_dim.2), calls=%async_computation | async-start | bytes 2097152 | tf_op jit(solution)/shard_map/all_to_all | solution.py:229
  35.5 0.0 all-gather.3.cloned.1.call-start
  35.6 0.0 copy-done.11
  35.6 0.1 copy.21
  35.7 0.0 copy-done.12
  35.7 0.7 pad_maximum_fusion.1
  36.4 0.0 all-gather.3.cloned.1.call-update
  36.4 0.0 reduce-scatter.2.cloned.1.call-start
  36.4 26.6 %all-to-all-done = bf16[8,2,128,256]{3,2,1,0:T(8,128)(2,1)S(1)} async-done(((bf16[8,2,128,256]{3,2,1,0:T(8,128)(2,1)}), bf16[8,2,128,256]{3,2,1,0:T(8,128)(2,1)S(1)}, u32[]{:S(2)}, u32[]{:S(2)}) %all-to-all-start) | async-done | bytes 1048608 | tf_op jit(solution)/shard_map/all_to_all | solution.py:229
  63.1 1.9 collective-permute-start.2
  65.0 17.5 %all-gather.3.cloned.1.call-done = bf16[16,128,256]{2,1,0:T(8,128)(2,1)} async-done(((bf16[2,128,256]{2,1,0:T(8,128)(2,1)}), bf16[16,128,256]{2,1,0:T(8,128)(2,1)}) %all-gather.3.cloned.1.call-update) | async-done | bytes 1048592 | tf_op jit(solution)/shard_map/all_gather | solution.py:226
  82.5 0.0 collective-permute-done.2
  82.5 0.0 copy-done.2
  82.5 0.0 copy-done.3
  82.5 0.0 copy-start
  82.5 1.2 copy-done
  83.7 0.8 shard_map.155
  84.5 0.0 copy-start.4
  84.6 0.0 copy-start.5
  84.6 0.0 copy-start.6
  84.6 0.0 copy-start.7
  84.6 0.0 copy-start.8
  84.6 0.0 copy-start.9
  84.6 20.8 %all_to_all.20.got = bf16[32,8,1280]{2,1,0:T(8,128)(2,1)S(1)} all-to-all(bf16[32,8,1280]{2,1,0:T(8,128)(2,1)S(1)} %bitcast.29), channel_id=1, replica_groups=mesh['x'=4,'y'=8,'zh'=4,'zl'=2,'core'=2] {'x','y'}, dimensions={0} | all-to-all | bytes 1310720 | tf_op jit(solution)/shard_map/all_to_all | solution.py:241
  105.4 0.0 copy-done.4
  105.4 0.0 copy-done.5
  105.4 0.0 copy-done.6
  105.4 0.0 copy-done.7
  105.4 0.0 copy-done.8
  105.5 0.0 copy-done.9
  105.5 1.3 shard_map.156
  106.8 0.0 copy-start.1
  106.8 20.1 %all_to_all.21 = bf16[32,8,1152]{2,1,0:T(8,128)(2,1)S(1)} all-to-all(bf16[32,8,1152]{2,1,0:T(8,128)(2,1)S(1)} %shard_map.156), channel_id=1, replica_groups=mesh['x'=4,'y'=8,'zh'=4,'zl'=2,'core'=2] {'x','y'}, dimensions={0} | all-to-all | bytes 1179648 | tf_op jit(solution)/shard_map/all_to_all | solution.py:260
  126.9 0.1 slice.24.got
  127.0 0.0 copy-done.1
  127.0 1.7 shard_map.157
  128.7 0.0 copy-done.10
  128.7 1.9 collective-permute-start.3
  130.7 1.7 shard_map.158
  132.4 0.0 reduce-scatter.2.cloned.1.call-update
  132.4 1.2 collective-permute-done.3
  133.6 2.5 %add_convert_fusion = bf16[4,2,2,128,256]{4,3,2,1,0:T(8,128)(2,1)} fusion(bf16[4,2,2,128,256]{4,3,2,1,0:T(8,128)(2,1)} %collective-permute-done.3, bf16[4,2,2,128,256]{4,3,2,1,0:T(8,128)(2,1)S(1)} %get-tuple-element.7), kind=kLoop, calls=%fused_computation | loop fusion | flops 2097152 | bytes 3145728 | tf_op jit(solution)/shard_map/convert_element_type | solution.py:278
  136.1 7.6 %all-to-all-start.3 = ((bf16[8,2,128,256]{3,2,1,0:T(8,128)(2,1)}), bf16[8,2,128,256]{3,2,1,0:T(8,128)(2,1)S(1)}, u32[]{:S(2)}, u32[]{:S(2)}) async-start(bf16[8,2,128,256]{3,2,1,0:T(8,128)(2,1)} %bitcast.11), calls=%async_computation.3 | async-start | bytes 2097152 | tf_op jit(solution)/shard_map/all_to_all | solution.py:279
  143.7 0.8 slice_bitcast_fusion.2
  144.5 0.7 copy.22
  145.3 27.5 %all-to-all-done.3 = bf16[8,2,128,256]{3,2,1,0:T(8,128)(2,1)S(1)} async-done(((bf16[8,2,128,256]{3,2,1,0:T(8,128)(2,1)}), bf16[8,2,128,256]{3,2,1,0:T(8,128)(2,1)S(1)}, u32[]{:S(2)}, u32[]{:S(2)}) %all-to-all-start.3) | async-done | bytes 1048608 | tf_op jit(solution)/shard_map/all_to_all | solution.py:279
  172.8 0.1 reduce_sum.12
  172.9 4.6 %collective-permute-start.5 = (bf16[128,256]{1,0:T(8,128)(2,1)S(1)}, bf16[128,256]{1,0:T(8,128)(2,1)S(1)}, u32[]{:S(2)}, u32[]{:S(2)}) collective-permute-start(bf16[128,256]{1,0:T(8,128)(2,1)S(1)} %get-tuple-element.21), channel_id=1, source_target_pairs={{0,0},{1,1},{2,2},{3,3},{4,128},{5,129},{6,130},{7,131},{8,256},{9... | collective-permute-start | bytes 196616 | tf_op jit(solution)/shard_map/ppermute | solution.py:284
  177.6 7.5 %collective-permute-start.4 = (bf16[128,256]{1,0:T(8,128)(2,1)S(1)}, bf16[128,256]{1,0:T(8,128)(2,1)S(1)}, u32[]{:S(2)}, u32[]{:S(2)}) collective-permute-start(bf16[128,256]{1,0:T(8,128)(2,1)S(1)} %get-tuple-element.22), channel_id=1, source_target_pairs={{0,0},{1,1},{2,2},{3,3},{4,128},{5,129},{6,130},{7,131},{8,256},{9... | collective-permute-start | bytes 196616 | tf_op jit(solution)/shard_map/ppermute | solution.py:283
  185.1 0.0 reduce-scatter.2.cloned.1.call-done
  185.1 1.5 slice_bitcast_fusion
  186.6 0.7 copy.23
  187.4 0.0 collective-permute-done.5
  187.4 2.7 %collective-permute-done.4 = bf16[128,256]{1,0:T(8,128)(2,1)S(1)} collective-permute-done((bf16[128,256]{1,0:T(8,128)(2,1)S(1)}, bf16[128,256]{1,0:T(8,128)(2,1)S(1)}, u32[]{:S(2)}, u32[]{:S(2)}) %collective-permute-start.4) | collective-permute-done | bytes 65568 | tf_op jit(solution)/shard_map/ppermute | solution.py:283
  190.1 0.6 copy.26
  190.7 0.6 copy.27
  (4 shorter events, 0.0 us)
Async XLA Ops:
  7.2 13.9 %collective-permute-start = (bf16[128,256]{1,0:T(8,128)(2,1)}, bf16[128,256]{1,0:T(8,128)(2,1)S(1)}, u32[]{:S(2)}, u32[]{:S(2)}) collective-permute-start(bf16[128,256]{1,0:T(8,128)(2,1)} %param.12), channel_id=1, source_target_pairs={{0,0},{1,1},{2,2},{3,3},{4,128},{5,129},{6,130},{7,131},{8,256},{9... | collective-permute-start | bytes 196616 | tf_op jit(solution)/shard_map/ppermute | solution.py:227
  18.0 12.7 %collective-permute-start.1 = (bf16[128,256]{1,0:T(8,128)(2,1)}, bf16[128,256]{1,0:T(8,128)(2,1)S(1)}, u32[]{:S(2)}, u32[]{:S(2)}) collective-permute-start(bf16[128,256]{1,0:T(8,128)(2,1)} %param.17), channel_id=1, source_target_pairs={{0,0},{1,1},{2,2},{3,3},{4,128},{5,129},{6,130},{7,131},{8,256},{9... | collective-permute-start | bytes 196616 | tf_op jit(solution)/shard_map/ppermute | solution.py:227
  31.8 3.8 %copy-start.11 = (bf16[256,128]{1,0:T(8,128)(2,1)S(1)}, bf16[256,128]{1,0:T(8,128)(2,1)}, u32[]{:S(2)}) copy-start(bf16[256,128]{1,0:T(8,128)(2,1)} %param.16) | copy-start | bytes 196612
  31.8 3.9 %copy-start.12 = (bf16[128,256]{1,0:T(8,128)(2,1)S(1)}, bf16[128,256]{1,0:T(8,128)(2,1)}, u32[]{:S(2)}) copy-start(bf16[128,256]{1,0:T(8,128)(2,1)} %param.15) | copy-start | bytes 196612
  31.8 50.7 %copy-start.2 = (bf16[128,256]{1,0:T(8,128)(2,1)S(1)}, bf16[128,256]{1,0:T(8,128)(2,1)}, u32[]{:S(2)}) copy-start(bf16[128,256]{1,0:T(8,128)(2,1)} %filters.1) | copy-start | bytes 196612
  31.8 50.7 %copy-start.3 = (bf16[128,256]{1,0:T(8,128)(2,1)S(1)}, bf16[128,256]{1,0:T(8,128)(2,1)}, u32[]{:S(2)}) copy-start(bf16[128,256]{1,0:T(8,128)(2,1)} %gate.1) | copy-start | bytes 196612
  31.8 31.2 %all-to-all-start = ((bf16[8,2,128,256]{3,2,1,0:T(8,128)(2,1)}), bf16[8,2,128,256]{3,2,1,0:T(8,128)(2,1)S(1)}, u32[]{:S(2)}, u32[]{:S(2)}) async-start(bf16[8,2,128,256]{3,2,1,0:T(8,128)(2,1)} %broadcast_in_dim.2), calls=%async_computation | async-start | bytes 2097152 | tf_op jit(solution)/shard_map/all_to_all | solution.py:229
  35.5 46.9 %all-gather.3.cloned.1.call-start = ((), (), s32[]{:S(2)}) async-start(), calls=%async_computation.6 | async-start | bytes 1179648 | tf_op jit(solution)/shard_map/all_gather | solution.py:226
  36.4 148.7 %reduce-scatter.2.cloned.1.call-start = ((), (), s32[]{:S(2)}) async-start(), calls=%async_computation.5 | async-start | bytes 1179648 | tf_op jit(solution)/shard_map/reduce_scatter | solution.py:270
  63.1 19.4 %collective-permute-start.2 = (bf16[8,2,128,256]{3,2,1,0:T(8,128)(2,1)S(1)}, bf16[8,2,128,256]{3,2,1,0:T(8,128)(2,1)S(1)}, u32[]{:S(2)}, u32[]{:S(2)}) collective-permute-start(bf16[8,2,128,256]{3,2,1,0:T(8,128)(2,1)S(1)} %all-to-all-done), channel_id=1, source_target_pairs={{0,1},{1,0},{2,3},{3,2},{4,5},{5,4},{6,7},{7,6},{8,9},{9,8},{10,11... | collective-permute-start | bytes 3145736 | tf_op jit(solution)/shard_map/ppermute | solution.py:230
  82.5 1.2 copy-start
  84.5 20.9 %copy-start.4 = (bf16[256,256]{1,0:T(8,128)(2,1)S(1)}, bf16[256,256]{1,0:T(8,128)(2,1)}, u32[]{:S(2)}) copy-start(bf16[256,256]{1,0:T(8,128)(2,1)} %constant.24.clone.second_back) | copy-start | bytes 393220
  84.6 20.9 %copy-start.5 = (bf16[256,256]{1,0:T(8,128)(2,1)S(1)}, bf16[256,256]{1,0:T(8,128)(2,1)}, u32[]{:S(2)}) copy-start(bf16[256,256]{1,0:T(8,128)(2,1)} %constant.23.clone.second) | copy-start | bytes 393220
  84.6 20.9 %copy-start.6 = (f32[64,128]{1,0:T(8,128)S(1)}, f32[64,128]{1,0:T(8,128)}, u32[]{:S(2)}) copy-start(f32[64,128]{1,0:T(8,128)} %constant.22.clone.twist_sin) | copy-start | bytes 98308
  84.6 20.9 %copy-start.7 = (f32[64,128]{1,0:T(8,128)S(1)}, f32[64,128]{1,0:T(8,128)}, u32[]{:S(2)}) copy-start(f32[64,128]{1,0:T(8,128)} %constant.21.clone.twist_cos) | copy-start | bytes 98308
  84.6 20.9 %copy-start.8 = (bf16[128,32]{1,0:T(8,128)(2,1)S(1)}, bf16[128,32]{1,0:T(8,128)(2,1)}, u32[]{:S(2)}) copy-start(bf16[128,32]{1,0:T(8,128)(2,1)} %constant.19.clone.first) | copy-start | bytes 24580
  84.6 20.9 %copy-start.9 = (bf16[32,128]{1,0:T(8,128)(2,1)S(1)}, bf16[32,128]{1,0:T(8,128)(2,1)}, u32[]{:S(2)}) copy-start(bf16[32,128]{1,0:T(8,128)(2,1)} %constant.20.clone.first_back) | copy-start | bytes 24580
  106.8 20.2 %copy-start.1 = (bf16[16,128,256]{2,1,0:T(8,128)(2,1)S(1)}, bf16[16,128,256]{2,1,0:T(8,128)(2,1)}, u32[]{:S(2)}) copy-start(bf16[16,128,256]{2,1,0:T(8,128)(2,1)} %all-gather.3.cloned.1.call-done) | copy-start | bytes 3145732
  126.9 1.8 copy-start.10
  128.7 4.9 %collective-permute-start.3 = (bf16[4,2,2,128,256]{4,3,2,1,0:T(8,128)(2,1)}, bf16[4,2,2,128,256]{4,3,2,1,0:T(8,128)(2,1)}, u32[]{:S(2)}, u32[]{:S(2)}) collective-permute-start(bf16[4,2,2,128,256]{4,3,2,1,0:T(8,128)(2,1)} %get-tuple-element.8), channel_id=1, source_target_pairs={{0,1},{1,0},{2,3},{3,2},{4,5},{5,4},{6,7},{7,6},{8,9},{9,8},{10,11... | collective-permute-start | bytes 3145736 | tf_op jit(solution)/shard_map/ppermute | solution.py:277
  136.1 36.6 %all-to-all-start.3 = ((bf16[8,2,128,256]{3,2,1,0:T(8,128)(2,1)}), bf16[8,2,128,256]{3,2,1,0:T(8,128)(2,1)S(1)}, u32[]{:S(2)}, u32[]{:S(2)}) async-start(bf16[8,2,128,256]{3,2,1,0:T(8,128)(2,1)} %bitcast.11), calls=%async_computation.3 | async-start | bytes 2097152 | tf_op jit(solution)/shard_map/all_to_all | solution.py:279
  172.9 14.5 %collective-permute-start.5 = (bf16[128,256]{1,0:T(8,128)(2,1)S(1)}, bf16[128,256]{1,0:T(8,128)(2,1)S(1)}, u32[]{:S(2)}, u32[]{:S(2)}) collective-permute-start(bf16[128,256]{1,0:T(8,128)(2,1)S(1)} %get-tuple-element.21), channel_id=1, source_target_pairs={{0,0},{1,1},{2,2},{3,3},{4,128},{5,129},{6,130},{7,131},{8,256},{9... | collective-permute-start | bytes 196616 | tf_op jit(solution)/shard_map/ppermute | solution.py:284
  177.6 12.5 %collective-permute-start.4 = (bf16[128,256]{1,0:T(8,128)(2,1)S(1)}, bf16[128,256]{1,0:T(8,128)(2,1)S(1)}, u32[]{:S(2)}, u32[]{:S(2)}) collective-permute-start(bf16[128,256]{1,0:T(8,128)(2,1)S(1)} %get-tuple-element.22), channel_id=1, source_target_pairs={{0,0},{1,1},{2,2},{3,3},{4,128},{5,129},{6,130},{7,131},{8,256},{9... | collective-permute-start | bytes 196616 | tf_op jit(solution)/shard_map/ppermute | solution.py:283
Sparse Core Ops, SparseCore 0:
  38.4 43.9 all-gather.2
  132.5 39.3 reduce-scatter.1

commit v2 on v1

--- a/solution.py
+++ b/solution.py
@@ -223,10 +223,14 @@
     me = lax.axis_index("core").astype(jnp.int32).reshape(1)
     swap = swap_pairs()
 
-    weights = lax.all_gather(jnp.stack([input_weight, output_weight.T]), "y", axis=0)
-    moved = jnp.stack([lax.ppermute(tokens, ALL, swap), lax.ppermute(cotangent, ALL, swap)])
+    pair, rows = lax.optimization_barrier(
+        (jnp.stack([input_weight, output_weight.T]), jnp.stack([tokens, cotangent]))
+    )
+    weights = lax.all_gather(pair, "y", axis=0)
+    moved = lax.ppermute(rows, ALL, swap)
     copies = jnp.broadcast_to(moved[None], (NH * NL, 2, tokens_here, features))
     own = lax.all_to_all(copies, Z, split_axis=0, concat_axis=0, tiled=True)
+    own, weights = lax.optimization_barrier((own, weights))
     other = lax.ppermute(own, "core", [(0, 1), (1, 0)])
     held = (NH, NL, 2, tokens_here, features)
     own, other = own.reshape(held), other.reshape(held)
@@ -280,9 +284,8 @@
         parts.reshape(NH * NL, 2, tokens_here, features), Z, split_axis=0, concat_axis=0, tiled=True
     )
     total = jnp.sum(parts.astype(f32), 0).astype(bf16)
-    layer_output = lax.ppermute(total[0], ALL, swap)
-    grad_tokens = lax.ppermute(total[1], ALL, swap)
-    return (layer_output, grad_tokens, grad_gate, grad_input_weight, grad_output_weight)
+    total = lax.ppermute(total, ALL, swap)
+    return (total[0], total[1], grad_gate, grad_input_weight, grad_output_weight)
 
 
 def solution(mesh):

time: 199 us -> 191 us (0.960)
  the two profiles are of different devices: /device:TPU:4 before, /device:TPU:10 now
where the time goes in v2:
time: 191 us
  waiting for transfers between devices  76.8 us (40%)
  blocking collectives  52.2 us (27%)
  starting transfers between devices  29.8 us (16%)
  between operations  14.2 us (7%)
  local copies, waits for them, and re-layouts  7.84 us (4%)
  Pallas kernels  5.6 us (3%)
  other arithmetic  4.25 us (2%)
    all_to_all x1, blocking collectives, on_device(): lax.all_to_all(sent.reshape(BLOCKS, OWN, 2 * half + 2 * ROWS), CTX, split...  28.6 us
    all_to_all x1, waiting for transfers between devices, on_device(): lax.all_to_all(parts.reshape(NH * NL, 2, tokens_here, features), Z, split...  27.7 us
    all_gather x1, waiting for transfers between devices, on_device(): weights = lax.all_gather(pair, 'y', axis=0)  23.8 us
    all_to_all x1, blocking collectives, on_device(): got = lax.all_to_all(sent, CTX, split_axis=0, concat_axis=0, tiled=True)  23.6 us
    all_to_all x1, starting transfers between devices, on_device(): own = lax.all_to_all(copies, Z, split_axis=0, concat_axis=0, tiled=True)  13.1 us
    ppermute x1, waiting for transfers between devices, on_device(): total = lax.ppermute(total, ALL, swap)  9.33 us
    ppermute x1, waiting for transfers between devices, on_device(): moved = lax.ppermute(rows, ALL, swap)  6.98 us
    ppermute x1, starting transfers between devices, on_device(): moved = lax.ppermute(rows, ALL, swap)  6.05 us
  transfers between devices with their start and end apart: 8, of which 7 were waited for; matrix products, arithmetic and copies ran while one was open for 4% of the time, Pallas kernels for 1%

profile of v2, /device:TPU:10, one launch (start us, length us, event | category | flops | bytes accessed | tf_op | source)
XLA Modules:
  0.0 190.7 jit_solution(1022560591053786490)
XLA Ops:
  7.2 0.0 all-gather.3.cloned.1.call-start
  7.2 0.9 copy.21
  8.2 1.6 pad_maximum_fusion
  9.7 6.0 %collective-permute-start = (bf16[2,128,256]{2,1,0:T(8,128)(2,1)S(1)}, bf16[2,128,256]{2,1,0:T(8,128)(2,1)S(1)}, u32[]{:S(2)}, u32[]{:S(2)}) collective-permute-start(bf16[2,128,256]{2,1,0:T(8,128)(2,1)S(1)} %get-tuple-element.11), channel_id=1, source_target_pairs={{0,0},{1,1},{2,2},{3,3},{4,128},{5,129},{6,130},{7,131},{8,256},{9... | collective-permute-start | bytes 393224 | tf_op jit(solution)/shard_map/ppermute | solution.py:230
  15.8 0.0 all-gather.3.cloned.1.call-update
  15.8 7.0 %collective-permute-done = bf16[2,128,256]{2,1,0:T(8,128)(2,1)S(1)} collective-permute-done((bf16[2,128,256]{2,1,0:T(8,128)(2,1)S(1)}, bf16[2,128,256]{2,1,0:T(8,128)(2,1)S(1)}, u32[]{:S(2)}, u32[]{:S(2)}) %collective-permute-start) | collective-permute-done | bytes 131104 | tf_op jit(solution)/shard_map/ppermute | solution.py:230
  22.8 1.1 broadcast_in_dim.2
  23.9 0.0 copy-start.2
  23.9 0.0 copy-start.3
  23.9 13.1 %all-to-all-start = ((bf16[8,2,128,256]{3,2,1,0:T(8,128)(2,1)}), bf16[8,2,128,256]{3,2,1,0:T(8,128)(2,1)S(1)}, u32[]{:S(2)}, u32[]{:S(2)}) async-start(bf16[8,2,128,256]{3,2,1,0:T(8,128)(2,1)} %broadcast_in_dim.2), calls=%async_computation | async-start | bytes 2097152 | tf_op jit(solution)/shard_map/all_to_all | solution.py:232
  37.0 0.0 reduce-scatter.2.cloned.1.call-start
  37.0 23.8 %all-gather.3.cloned.1.call-done = bf16[16,128,256]{2,1,0:T(8,128)(2,1)} async-done(((bf16[2,128,256]{2,1,0:T(8,128)(2,1)}), bf16[16,128,256]{2,1,0:T(8,128)(2,1)}) %all-gather.3.cloned.1.call-update) | async-done | bytes 1048592 | tf_op jit(solution)/shard_map/all_gather | solution.py:229
  60.8 5.1 %all-to-all-done = bf16[8,2,128,256]{3,2,1,0:T(8,128)(2,1)S(1)} async-done(((bf16[8,2,128,256]{3,2,1,0:T(8,128)(2,1)}), bf16[8,2,128,256]{3,2,1,0:T(8,128)(2,1)S(1)}, u32[]{:S(2)}, u32[]{:S(2)}) %all-to-all-start) | async-done | bytes 1048608 | tf_op jit(solution)/shard_map/all_to_all | solution.py:232
  65.9 1.9 %collective-permute-start.1 = (bf16[8,2,128,256]{3,2,1,0:T(8,128)(2,1)S(1)}, bf16[8,2,128,256]{3,2,1,0:T(8,128)(2,1)S(1)}, u32[]{:S(2)}, u32[]{:S(2)}) collective-permute-start(bf16[8,2,128,256]{3,2,1,0:T(8,128)(2,1)S(1)} %all-to-all-done), channel_id=1, source_target_pairs={{0,1},{1,0},{2,3},{3,2},{4,5},{5,4},{6,7},{7,6},{8,9},{9,8},{10,11... | collective-permute-start | bytes 3145736 | tf_op jit(solution)/shard_map/ppermute | solution.py:234
  67.9 2.6 %collective-permute-done.1 = bf16[8,2,128,256]{3,2,1,0:T(8,128)(2,1)S(1)} collective-permute-done((bf16[8,2,128,256]{3,2,1,0:T(8,128)(2,1)S(1)}, bf16[8,2,128,256]{3,2,1,0:T(8,128)(2,1)S(1)}, u32[]{:S(2)}, u32[]{:S(2)}) %collective-permute-start.1) | collective-permute-done | bytes 1048608 | tf_op jit(solution)/shard_map/ppermute | solution.py:234
  70.5 0.0 copy-done.2
  70.5 0.0 copy-done.3
  70.5 0.0 copy-start
  70.5 1.2 copy-done
  71.7 0.8 shard_map.155
  72.6 0.0 copy-start.4
  72.6 0.0 copy-start.5
  72.6 0.0 copy-start.6
  72.6 0.0 copy-start.7
  72.6 0.0 copy-start.8
  72.6 0.0 copy-start.9
  72.6 28.6 %all_to_all.20.got = bf16[32,8,1280]{2,1,0:T(8,128)(2,1)S(1)} all-to-all(bf16[32,8,1280]{2,1,0:T(8,128)(2,1)S(1)} %bitcast.29), channel_id=1, replica_groups=mesh['x'=4,'y'=8,'zh'=4,'zl'=2,'core'=2] {'x','y'}, dimensions={0} | all-to-all | bytes 1310720 | tf_op jit(solution)/shard_map/all_to_all | solution.py:245
  101.3 0.0 copy-done.4
  101.3 0.0 copy-done.5
  101.3 0.0 copy-done.6
  101.3 0.0 copy-done.7
  101.3 0.0 copy-done.8
  101.3 0.0 copy-done.9
  101.3 1.3 shard_map.156
  102.6 0.0 copy-start.1
  102.6 23.6 %all_to_all.21 = bf16[32,8,1152]{2,1,0:T(8,128)(2,1)S(1)} all-to-all(bf16[32,8,1152]{2,1,0:T(8,128)(2,1)S(1)} %shard_map.156), channel_id=1, replica_groups=mesh['x'=4,'y'=8,'zh'=4,'zl'=2,'core'=2] {'x','y'}, dimensions={0} | all-to-all | bytes 1179648 | tf_op jit(solution)/shard_map/all_to_all | solution.py:264
  126.2 0.0 copy-start.10
  126.2 0.1 slice.24.got
  126.2 0.0 copy-done.1
  126.2 1.7 shard_map.157
  128.0 0.0 copy-done.10
  128.0 1.9 %collective-permute-start.2 = (bf16[4,2,2,128,256]{4,3,2,1,0:T(8,128)(2,1)}, bf16[4,2,2,128,256]{4,3,2,1,0:T(8,128)(2,1)}, u32[]{:S(2)}, u32[]{:S(2)}) collective-permute-start(bf16[4,2,2,128,256]{4,3,2,1,0:T(8,128)(2,1)} %get-tuple-element.16), channel_id=1, source_target_pairs={{0,1},{1,0},{2,3},{3,2},{4,5},{5,4},{6,7},{7,6},{8,9},{9,8},{10,11... | collective-permute-start | bytes 3145736 | tf_op jit(solution)/shard_map/ppermute | solution.py:281
  129.9 1.7 shard_map.158
  131.6 0.0 reduce-scatter.2.cloned.1.call-update
  131.6 1.2 collective-permute-done.2
  132.9 2.5 %add_convert_fusion = bf16[4,2,2,128,256]{4,3,2,1,0:T(8,128)(2,1)} fusion(bf16[4,2,2,128,256]{4,3,2,1,0:T(8,128)(2,1)} %collective-permute-done.2, bf16[4,2,2,128,256]{4,3,2,1,0:T(8,128)(2,1)S(1)} %get-tuple-element.15), kind=kLoop, calls=%fused_computation | loop fusion | flops 2097152 | bytes 3145728 | tf_op jit(solution)/shard_map/convert_element_type | solution.py:282
  135.4 3.6 %all-to-all-start.3 = ((bf16[8,2,128,256]{3,2,1,0:T(8,128)(2,1)}), bf16[8,2,128,256]{3,2,1,0:T(8,128)(2,1)S(1)}, u32[]{:S(2)}, u32[]{:S(2)}) async-start(bf16[8,2,128,256]{3,2,1,0:T(8,128)(2,1)} %bitcast.11), calls=%async_computation.3 | async-start | bytes 2097152 | tf_op jit(solution)/shard_map/all_to_all | solution.py:283
  139.0 0.8 slice_bitcast_fusion.2
  139.8 0.7 copy.22
  140.5 27.7 %all-to-all-done.3 = bf16[8,2,128,256]{3,2,1,0:T(8,128)(2,1)S(1)} async-done(((bf16[8,2,128,256]{3,2,1,0:T(8,128)(2,1)}), bf16[8,2,128,256]{3,2,1,0:T(8,128)(2,1)S(1)}, u32[]{:S(2)}, u32[]{:S(2)}) %all-to-all-start.3) | async-done | bytes 1048608 | tf_op jit(solution)/shard_map/all_to_all | solution.py:283
  168.3 0.1 reduce_sum.12
  168.4 3.2 %collective-permute-start.3 = (bf16[2,128,256]{2,1,0:T(8,128)(2,1)S(1)}, bf16[2,128,256]{2,1,0:T(8,128)(2,1)S(1)}, u32[]{:S(2)}, u32[]{:S(2)}) collective-permute-start(bf16[2,128,256]{2,1,0:T(8,128)(2,1)S(1)} %reduce_sum.12), channel_id=1, source_target_pairs={{0,0},{1,1},{2,2},{3,3},{4,128},{5,129},{6,130},{7,131},{8,256},{9... | collective-permute-start | bytes 393224 | tf_op jit(solution)/shard_map/ppermute | solution.py:287
  171.6 0.0 reduce-scatter.2.cloned.1.call-done
  171.6 1.5 slice_bitcast_fusion
  173.1 0.7 copy.23
  173.9 9.3 %collective-permute-done.3 = bf16[2,128,256]{2,1,0:T(8,128)(2,1)S(1)} collective-permute-done((bf16[2,128,256]{2,1,0:T(8,128)(2,1)S(1)}, bf16[2,128,256]{2,1,0:T(8,128)(2,1)S(1)}, u32[]{:S(2)}, u32[]{:S(2)}) %collective-permute-start.3) | collective-permute-done | bytes 131104 | tf_op jit(solution)/shard_map/ppermute | solution.py:287
  183.2 0.7 slice_bitcast_fusion.3
Async XLA Ops:
  7.2 53.6 %all-gather.3.cloned.1.call-start = ((), (), s32[]{:S(2)}) async-start(), calls=%async_computation.6 | async-start | bytes 1179648 | tf_op jit(solution)/shard_map/all_gather | solution.py:229
  9.7 13.1 %collective-permute-start = (bf16[2,128,256]{2,1,0:T(8,128)(2,1)S(1)}, bf16[2,128,256]{2,1,0:T(8,128)(2,1)S(1)}, u32[]{:S(2)}, u32[]{:S(2)}) collective-permute-start(bf16[2,128,256]{2,1,0:T(8,128)(2,1)S(1)} %get-tuple-element.11), channel_id=1, source_target_pairs={{0,0},{1,1},{2,2},{3,3},{4,128},{5,129},{6,130},{7,131},{8,256},{9... | collective-permute-start | bytes 393224 | tf_op jit(solution)/shard_map/ppermute | solution.py:230
  23.9 46.6 %copy-start.2 = (bf16[128,256]{1,0:T(8,128)(2,1)S(1)}, bf16[128,256]{1,0:T(8,128)(2,1)}, u32[]{:S(2)}) copy-start(bf16[128,256]{1,0:T(8,128)(2,1)} %filters.1) | copy-start | bytes 196612
  23.9 46.6 %copy-start.3 = (bf16[128,256]{1,0:T(8,128)(2,1)S(1)}, bf16[128,256]{1,0:T(8,128)(2,1)}, u32[]{:S(2)}) copy-start(bf16[128,256]{1,0:T(8,128)(2,1)} %gate.1) | copy-start | bytes 196612
  23.9 42.1 %all-to-all-start = ((bf16[8,2,128,256]{3,2,1,0:T(8,128)(2,1)}), bf16[8,2,128,256]{3,2,1,0:T(8,128)(2,1)S(1)}, u32[]{:S(2)}, u32[]{:S(2)}) async-start(bf16[8,2,128,256]{3,2,1,0:T(8,128)(2,1)} %broadcast_in_dim.2), calls=%async_computation | async-start | bytes 2097152 | tf_op jit(solution)/shard_map/all_to_all | solution.py:232
  37.0 134.7 %reduce-scatter.2.cloned.1.call-start = ((), (), s32[]{:S(2)}) async-start(), calls=%async_computation.5 | async-start | bytes 1179648 | tf_op jit(solution)/shard_map/reduce_scatter | solution.py:274
  65.9 4.5 %collective-permute-start.1 = (bf16[8,2,128,256]{3,2,1,0:T(8,128)(2,1)S(1)}, bf16[8,2,128,256]{3,2,1,0:T(8,128)(2,1)S(1)}, u32[]{:S(2)}, u32[]{:S(2)}) collective-permute-start(bf16[8,2,128,256]{3,2,1,0:T(8,128)(2,1)S(1)} %all-to-all-done), channel_id=1, source_target_pairs={{0,1},{1,0},{2,3},{3,2},{4,5},{5,4},{6,7},{7,6},{8,9},{9,8},{10,11... | collective-permute-start | bytes 3145736 | tf_op jit(solution)/shard_map/ppermute | solution.py:234
  70.5 1.2 copy-start
  72.6 28.7 %copy-start.4 = (bf16[256,256]{1,0:T(8,128)(2,1)S(1)}, bf16[256,256]{1,0:T(8,128)(2,1)}, u32[]{:S(2)}) copy-start(bf16[256,256]{1,0:T(8,128)(2,1)} %constant.24.clone.second_back) | copy-start | bytes 393220
  72.6 28.7 %copy-start.5 = (bf16[256,256]{1,0:T(8,128)(2,1)S(1)}, bf16[256,256]{1,0:T(8,128)(2,1)}, u32[]{:S(2)}) copy-start(bf16[256,256]{1,0:T(8,128)(2,1)} %constant.23.clone.second) | copy-start | bytes 393220
  72.6 28.7 %copy-start.6 = (f32[64,128]{1,0:T(8,128)S(1)}, f32[64,128]{1,0:T(8,128)}, u32[]{:S(2)}) copy-start(f32[64,128]{1,0:T(8,128)} %constant.22.clone.twist_sin) | copy-start | bytes 98308
  72.6 28.7 %copy-start.7 = (f32[64,128]{1,0:T(8,128)S(1)}, f32[64,128]{1,0:T(8,128)}, u32[]{:S(2)}) copy-start(f32[64,128]{1,0:T(8,128)} %constant.21.clone.twist_cos) | copy-start | bytes 98308
  72.6 28.7 %copy-start.8 = (bf16[128,32]{1,0:T(8,128)(2,1)S(1)}, bf16[128,32]{1,0:T(8,128)(2,1)}, u32[]{:S(2)}) copy-start(bf16[128,32]{1,0:T(8,128)(2,1)} %constant.19.clone.first) | copy-start | bytes 24580
  72.6 28.7 %copy-start.9 = (bf16[32,128]{1,0:T(8,128)(2,1)S(1)}, bf16[32,128]{1,0:T(8,128)(2,1)}, u32[]{:S(2)}) copy-start(bf16[32,128]{1,0:T(8,128)(2,1)} %constant.20.clone.first_back) | copy-start | bytes 24580
  102.6 23.6 %copy-start.1 = (bf16[16,128,256]{2,1,0:T(8,128)(2,1)S(1)}, bf16[16,128,256]{2,1,0:T(8,128)(2,1)}, u32[]{:S(2)}) copy-start(bf16[16,128,256]{2,1,0:T(8,128)(2,1)} %all-gather.3.cloned.1.call-done) | copy-start | bytes 3145732
  126.2 1.8 copy-start.10
  128.0 4.9 %collective-permute-start.2 = (bf16[4,2,2,128,256]{4,3,2,1,0:T(8,128)(2,1)}, bf16[4,2,2,128,256]{4,3,2,1,0:T(8,128)(2,1)}, u32[]{:S(2)}, u32[]{:S(2)}) collective-permute-start(bf16[4,2,2,128,256]{4,3,2,1,0:T(8,128)(2,1)} %get-tuple-element.16), channel_id=1, source_target_pairs={{0,1},{1,0},{2,3},{3,2},{4,5},{5,4},{6,7},{7,6},{8,9},{9,8},{10,11... | collective-permute-start | bytes 3145736 | tf_op jit(solution)/shard_map/ppermute | solution.py:281
  135.4 32.9 %all-to-all-start.3 = ((bf16[8,2,128,256]{3,2,1,0:T(8,128)(2,1)}), bf16[8,2,128,256]{3,2,1,0:T(8,128)(2,1)S(1)}, u32[]{:S(2)}, u32[]{:S(2)}) async-start(bf16[8,2,128,256]{3,2,1,0:T(8,128)(2,1)} %bitcast.11), calls=%async_computation.3 | async-start | bytes 2097152 | tf_op jit(solution)/shard_map/all_to_all | solution.py:283
  168.4 14.8 %collective-permute-start.3 = (bf16[2,128,256]{2,1,0:T(8,128)(2,1)S(1)}, bf16[2,128,256]{2,1,0:T(8,128)(2,1)S(1)}, u32[]{:S(2)}, u32[]{:S(2)}) collective-permute-start(bf16[2,128,256]{2,1,0:T(8,128)(2,1)S(1)} %reduce_sum.12), channel_id=1, source_target_pairs={{0,0},{1,1},{2,2},{3,3},{4,128},{5,129},{6,130},{7,131},{8,256},{9... | collective-permute-start | bytes 393224 | tf_op jit(solution)/shard_map/ppermute | solution.py:287
Sparse Core Ops, SparseCore 0:
  15.9 44.8 all-gather.2
  131.8 32.4 reduce-scatter.1

commit v3 on v2

--- a/solution.py
+++ b/solution.py
@@ -21,6 +21,7 @@
 ROWS = 128
 FREQS = 2 * BLOCKS
 LENGTH = FREQS * ROWS
+SPARE = 16
 OWN = 8
 
 VMEM = pl.BlockSpec(memory_space=pltpu.VMEM)
@@ -68,18 +69,26 @@
 
 def weight_block(weights, which, l, c):
     first = 4 * l + 2 * c
-    return jnp.concatenate([weights[first, which], weights[first + 1, which]], 0)
-
-
-def project_kernel(me_ref, own, other, weights, filters, gate, out):
-    me = me_ref[0]
+    return jnp.concatenate([weights[first, which, :ROWS], weights[first + 1, which, :ROWS]], 0)
+
+
+def product_terms(held, weights, which, c):
+    total = None
+    for l in range(NL):
+        rows = held[:, l, which].reshape(NX * ROWS, 2 * ROWS)
+        term = dot(rows, weight_block(weights, which, l, c))
+        total = term if total is None else total + term
+    return total
+
+
+def project_own_kernel(me_ref, own, weights, totals):
     for which in range(2):
-        total = None
-        for l in range(NL):
-            for held, c in ((own, me), (other, 1 - me)):
-                rows = held[:, l, which].reshape(NX * ROWS, 2 * ROWS)
-                term = dot(rows, weight_block(weights, which, l, c))
-                total = term if total is None else total + term
+        totals[which] = product_terms(own, weights, which, me_ref[0])
+
+
+def project_kernel(me_ref, other, weights, totals, filters, gate, out):
+    for which in range(2):
+        total = totals[which] + product_terms(other, weights, which, 1 - me_ref[0])
         out[:, which * NX * ROWS : (which + 1) * NX * ROWS] = total.T.astype(bf16)
     base = 2 * NX * ROWS
     out[:, base : base + ROWS] = filters[...].astype(f32).T.astype(bf16)
@@ -226,21 +235,26 @@
     pair, rows = lax.optimization_barrier(
         (jnp.stack([input_weight, output_weight.T]), jnp.stack([tokens, cotangent]))
     )
-    weights = lax.all_gather(pair, "y", axis=0)
+    weights = lax.all_gather(jnp.pad(pair, ((0, 0), (0, SPARE), (0, 0))), "y", axis=0)
     moved = lax.ppermute(rows, ALL, swap)
     copies = jnp.broadcast_to(moved[None], (NH * NL, 2, tokens_here, features))
     own = lax.all_to_all(copies, Z, split_axis=0, concat_axis=0, tiled=True)
-    own, weights = lax.optimization_barrier((own, weights))
     other = lax.ppermute(own, "core", [(0, 1), (1, 0)])
     held = (NH, NL, 2, tokens_here, features)
     own, other = own.reshape(held), other.reshape(held)
 
     half = NX * ROWS
+    totals = call(
+        project_own_kernel,
+        (me, own, weights),
+        jax.ShapeDtypeStruct((2, half, channels), f32),
+        4 * half * 512 * channels,
+    )
     sent = call(
         project_kernel,
-        (me, own, other, weights, filters, gate_values),
+        (me, other, weights, totals, filters, gate_values),
         jax.ShapeDtypeStruct((channels, 2 * half + 2 * ROWS), bf16),
-        4 * half * 1024 * channels,
+        4 * half * 512 * channels,
     )
     got = lax.all_to_all(
         sent.reshape(BLOCKS, OWN, 2 * half + 2 * ROWS), CTX, split_axis=0, concat_axis=0, tiled=True

time: 191 us -> 197 us (1.031)
  waiting for transfers between devices: 76.8 us -> 87 us
  blocking collectives: 52.2 us -> 43.2 us
  starting transfers between devices: 29.8 us -> 33.2 us
    all_to_all x1, waiting for transfers between devices: 5.14 us -> 28.2 us  [on_device(): own = lax.all_to_all(copies, Z, split_axis=0, concat_axis=0, tiled=True)]
    all_gather x1, waiting for transfers between devices: 23.8 us -> 13.6 us  [on_device(): lax.all_gather(jnp.pad(pair, ((0, 0), (0, SPARE), (0, 0))), 'y', axis=0)]
    all_to_all x1, blocking collectives: 28.6 us -> 23.6 us  [on_device(): lax.all_to_all(sent.reshape(BLOCKS, OWN, 2 * half + 2 * ROWS), CTX, split...]
    all_to_all x1, blocking collectives: 23.6 us -> 19.6 us  [on_device(): got = lax.all_to_all(sent, CTX, split_axis=0, concat_axis=0, tiled=True)]
    all_to_all x1, starting transfers between devices: 3.56 us -> 7.25 us  [on_device(): lax.all_to_all(parts.reshape(NH * NL, 2, tokens_here, features), Z, split...]
    ppermute x1, waiting for transfers between devices: 2.62 us -> 0.01 us  [on_device(): other = lax.ppermute(own, 'core', [(0, 1), (1, 0)])]
    pallas_call x4 -> x5, Pallas kernels: 5.6 us -> 5.77 us  [call(): pl.pallas_call(kernel, out_shape=out_shape, in_specs=specs, out_specs=(VM...]
  transfers between devices with their start and end apart: 8 -> 8, of which waited for: 7 -> 6; matrix products, arithmetic and copies ran while one was open for 4% -> 4% of each run, Pallas kernels for 1% -> 1%
where the time goes in v3:
time: 197 us; the launch traced here: 196 us
  waiting for transfers between devices  87 us (44%)
  blocking collectives  43.2 us (22%)
  starting transfers between devices  33.2 us (17%)
  between operations  14.2 us (7%)
  local copies, waits for them, and re-layouts  8.96 us (5%)
  Pallas kernels  5.77 us (3%)
  other arithmetic  3.59 us (2%)
    all_to_all x1, waiting for transfers between devices, on_device(): own = lax.all_to_all(copies, Z, split_axis=0, concat_axis=0, tiled=True)  28.2 us
    all_to_all x1, waiting for transfers between devices, on_device(): lax.all_to_all(parts.reshape(NH * NL, 2, tokens_here, features), Z, split...  27.5 us
    all_to_all x1, blocking collectives, on_device(): lax.all_to_all(sent.reshape(BLOCKS, OWN, 2 * half + 2 * ROWS), CTX, split...  23.6 us
    all_to_all x1, blocking collectives, on_device(): got = lax.all_to_all(sent, CTX, split_axis=0, concat_axis=0, tiled=True)  19.6 us
    all_gather x1, waiting for transfers between devices, on_device(): lax.all_gather(jnp.pad(pair, ((0, 0), (0, SPARE), (0, 0))), 'y', axis=0)  13.6 us
    all_to_all x1, starting transfers between devices, on_device(): own = lax.all_to_all(copies, Z, split_axis=0, concat_axis=0, tiled=True)  13 us
    ppermute x1, waiting for transfers between devices, on_device(): total = lax.ppermute(total, ALL, swap)  9.54 us
    all_to_all x1, starting transfers between devices, on_device(): lax.all_to_all(parts.reshape(NH * NL, 2, tokens_here, features), Z, split...  7.25 us
  transfers between devices with their start and end apart: 8, of which 6 were waited for; matrix products, arithmetic and copies ran while one was open for 4% of the time, Pallas kernels for 1%

profile of v3, /device:TPU:10, one launch (start us, length us, event | category | flops | bytes accessed | tf_op | source)
XLA Modules:
  0.0 196.0 jit_solution(12438015599836606974)
XLA Ops:
  7.2 0.9 copy.21
  8.1 0.9 pad_maximum_fusion
  9.0 6.1 %collective-permute-start = (bf16[2,128,256]{2,1,0:T(8,128)(2,1)S(1)}, bf16[2,128,256]{2,1,0:T(8,128)(2,1)S(1)}, u32[]{:S(2)}, u32[]{:S(2)}) collective-permute-start(bf16[2,128,256]{2,1,0:T(8,128)(2,1)S(1)} %get-tuple-element.9), channel_id=1, source_target_pairs={{0,0},{1,1},{2,2},{3,3},{4,128},{5,129},{6,130},{7,131},{8,256},{9... | collective-permute-start | bytes 393224 | tf_op jit(solution)/shard_map/ppermute | solution.py:239
  15.1 7.0 %collective-permute-done = bf16[2,128,256]{2,1,0:T(8,128)(2,1)S(1)} collective-permute-done((bf16[2,128,256]{2,1,0:T(8,128)(2,1)S(1)}, bf16[2,128,256]{2,1,0:T(8,128)(2,1)S(1)}, u32[]{:S(2)}, u32[]{:S(2)}) %collective-permute-start) | collective-permute-done | bytes 131104 | tf_op jit(solution)/shard_map/ppermute | solution.py:239
  22.1 1.1 broadcast_in_dim.2
  23.2 13.0 %all-to-all-start = ((bf16[8,2,128,256]{3,2,1,0:T(8,128)(2,1)}), bf16[8,2,128,256]{3,2,1,0:T(8,128)(2,1)S(1)}, u32[]{:S(2)}, u32[]{:S(2)}) async-start(bf16[8,2,128,256]{3,2,1,0:T(8,128)(2,1)} %broadcast_in_dim.2), calls=%async_computation | async-start | bytes 2097152 | tf_op jit(solution)/shard_map/all_to_all | solution.py:241
  36.1 0.0 all-gather.3.cloned.1.call-start
  36.2 0.7 pad.4
  36.9 0.0 all-gather.3.cloned.1.call-update
  36.9 0.0 reduce-scatter.2.cloned.1.call-start
  36.9 28.2 %all-to-all-done = bf16[8,2,128,256]{3,2,1,0:T(8,128)(2,1)S(1)} async-done(((bf16[8,2,128,256]{3,2,1,0:T(8,128)(2,1)}), bf16[8,2,128,256]{3,2,1,0:T(8,128)(2,1)S(1)}, u32[]{:S(2)}, u32[]{:S(2)}) %all-to-all-start) | async-done | bytes 1048608 | tf_op jit(solution)/shard_map/all_to_all | solution.py:241
  65.1 1.9 collective-permute-start.1
  67.0 13.6 %all-gather.3.cloned.1.call-done = bf16[16,144,256]{2,1,0:T(8,128)(2,1)} async-done(((bf16[2,144,256]{2,1,0:T(8,128)(2,1)}), bf16[16,144,256]{2,1,0:T(8,128)(2,1)}) %all-gather.3.cloned.1.call-update) | async-done | bytes 1179664 | tf_op jit(solution)/shard_map/all_gather | solution.py:238
  80.6 0.0 copy-start
  80.6 1.3 copy-done
  81.9 0.0 copy-start.2
  81.9 0.0 copy-start.3
  81.9 0.4 shard_map.155.totals
  82.3 0.0 collective-permute-done.1
  82.3 0.4 copy-done.2
  82.7 0.0 copy-done.3
  82.7 0.6 shard_map.156
  83.3 0.0 copy-start.4
  83.3 0.0 copy-start.5
  83.3 0.0 copy-start.6
  83.4 0.0 copy-start.7
  83.4 0.0 copy-start.8
  83.4 0.0 copy-start.9
  83.4 23.6 %all_to_all.20.got = bf16[32,8,1280]{2,1,0:T(8,128)(2,1)S(1)} all-to-all(bf16[32,8,1280]{2,1,0:T(8,128)(2,1)S(1)} %bitcast.32), channel_id=1, replica_groups=mesh['x'=4,'y'=8,'zh'=4,'zl'=2,'core'=2] {'x','y'}, dimensions={0} | all-to-all | bytes 1310720 | tf_op jit(solution)/shard_map/all_to_all | solution.py:259
  107.0 0.0 copy-done.4
  107.0 0.0 copy-done.5
  107.0 0.0 copy-done.6
  107.0 0.0 copy-done.7
  107.0 0.0 copy-done.8
  107.0 0.0 copy-done.9
  107.0 1.3 shard_map.157
  108.3 0.0 copy-start.1
  108.4 19.6 %all_to_all.21 = bf16[32,8,1152]{2,1,0:T(8,128)(2,1)S(1)} all-to-all(bf16[32,8,1152]{2,1,0:T(8,128)(2,1)S(1)} %shard_map.157), channel_id=1, replica_groups=mesh['x'=4,'y'=8,'zh'=4,'zl'=2,'core'=2] {'x','y'}, dimensions={0} | all-to-all | bytes 1179648 | tf_op jit(solution)/shard_map/all_to_all | solution.py:278
  127.9 0.0 copy-start.10
  127.9 0.1 slice.24.got
  128.0 0.0 copy-done.1
  128.0 1.7 shard_map.158
  129.8 0.0 copy-done.10
  129.8 1.9 collective-permute-start.2
  131.7 1.7 shard_map.159
  133.4 0.0 reduce-scatter.2.cloned.1.call-update
  133.4 1.2 collective-permute-done.2
  134.7 2.5 %add_convert_fusion = bf16[4,2,2,128,256]{4,3,2,1,0:T(8,128)(2,1)} fusion(bf16[4,2,2,128,256]{4,3,2,1,0:T(8,128)(2,1)} %collective-permute-done.2, bf16[4,2,2,128,256]{4,3,2,1,0:T(8,128)(2,1)S(1)} %get-tuple-element.11), kind=kLoop, calls=%fused_computation | loop fusion | flops 2097152 | bytes 3145728 | tf_op jit(solution)/shard_map/convert_element_type | solution.py:296
  137.2 7.2 %all-to-all-start.3 = ((bf16[8,2,128,256]{3,2,1,0:T(8,128)(2,1)}), bf16[8,2,128,256]{3,2,1,0:T(8,128)(2,1)S(1)}, u32[]{:S(2)}, u32[]{:S(2)}) async-start(bf16[8,2,128,256]{3,2,1,0:T(8,128)(2,1)} %bitcast.11), calls=%async_computation.3 | async-start | bytes 2097152 | tf_op jit(solution)/shard_map/all_to_all | solution.py:297
  144.4 0.8 slice_bitcast_fusion.2
  145.3 0.7 copy.22
  146.0 27.5 %all-to-all-done.3 = bf16[8,2,128,256]{3,2,1,0:T(8,128)(2,1)S(1)} async-done(((bf16[8,2,128,256]{3,2,1,0:T(8,128)(2,1)}), bf16[8,2,128,256]{3,2,1,0:T(8,128)(2,1)S(1)}, u32[]{:S(2)}, u32[]{:S(2)}) %all-to-all-start.3) | async-done | bytes 1048608 | tf_op jit(solution)/shard_map/all_to_all | solution.py:297
  173.5 0.1 reduce_sum.12
  173.7 3.1 %collective-permute-start.3 = (bf16[2,128,256]{2,1,0:T(8,128)(2,1)S(1)}, bf16[2,128,256]{2,1,0:T(8,128)(2,1)S(1)}, u32[]{:S(2)}, u32[]{:S(2)}) collective-permute-start(bf16[2,128,256]{2,1,0:T(8,128)(2,1)S(1)} %reduce_sum.12), channel_id=1, source_target_pairs={{0,0},{1,1},{2,2},{3,3},{4,128},{5,129},{6,130},{7,131},{8,256},{9... | collective-permute-start | bytes 393224 | tf_op jit(solution)/shard_map/ppermute | solution.py:301
  176.7 0.0 reduce-scatter.2.cloned.1.call-done
  176.7 1.5 slice_bitcast_fusion
  178.3 0.7 copy.23
  179.0 9.5 %collective-permute-done.3 = bf16[2,128,256]{2,1,0:T(8,128)(2,1)S(1)} collective-permute-done((bf16[2,128,256]{2,1,0:T(8,128)(2,1)S(1)}, bf16[2,128,256]{2,1,0:T(8,128)(2,1)S(1)}, u32[]{:S(2)}, u32[]{:S(2)}) %collective-permute-start.3) | collective-permute-done | bytes 131104 | tf_op jit(solution)/shard_map/ppermute | solution.py:301
  188.5 0.7 slice_bitcast_fusion.3
Async XLA Ops:
  9.0 13.1 %collective-permute-start = (bf16[2,128,256]{2,1,0:T(8,128)(2,1)S(1)}, bf16[2,128,256]{2,1,0:T(8,128)(2,1)S(1)}, u32[]{:S(2)}, u32[]{:S(2)}) collective-permute-start(bf16[2,128,256]{2,1,0:T(8,128)(2,1)S(1)} %get-tuple-element.9), channel_id=1, source_target_pairs={{0,0},{1,1},{2,2},{3,3},{4,128},{5,129},{6,130},{7,131},{8,256},{9... | collective-permute-start | bytes 393224 | tf_op jit(solution)/shard_map/ppermute | solution.py:239
  23.2 41.9 %all-to-all-start = ((bf16[8,2,128,256]{3,2,1,0:T(8,128)(2,1)}), bf16[8,2,128,256]{3,2,1,0:T(8,128)(2,1)S(1)}, u32[]{:S(2)}, u32[]{:S(2)}) async-start(bf16[8,2,128,256]{3,2,1,0:T(8,128)(2,1)} %broadcast_in_dim.2), calls=%async_computation | async-start | bytes 2097152 | tf_op jit(solution)/shard_map/all_to_all | solution.py:241
  36.1 44.4 %all-gather.3.cloned.1.call-start = ((), (), s32[]{:S(2)}) async-start(), calls=%async_computation.6 | async-start | bytes 1327104 | tf_op jit(solution)/shard_map/all_gather | solution.py:238
  36.9 139.9 %reduce-scatter.2.cloned.1.call-start = ((), (), s32[]{:S(2)}) async-start(), calls=%async_computation.5 | async-start | bytes 1179648 | tf_op jit(solution)/shard_map/reduce_scatter | solution.py:288
  65.1 17.2 %collective-permute-start.1 = (bf16[8,2,128,256]{3,2,1,0:T(8,128)(2,1)S(1)}, bf16[8,2,128,256]{3,2,1,0:T(8,128)(2,1)S(1)}, u32[]{:S(2)}, u32[]{:S(2)}) collective-permute-start(bf16[8,2,128,256]{3,2,1,0:T(8,128)(2,1)S(1)} %all-to-all-done), channel_id=1, source_target_pairs={{0,1},{1,0},{2,3},{3,2},{4,5},{5,4},{6,7},{7,6},{8,9},{9,8},{10,11... | collective-permute-start | bytes 3145736 | tf_op jit(solution)/shard_map/ppermute | solution.py:242
  80.6 1.3 copy-start
  81.9 0.8 copy-start.2
  81.9 0.9 copy-start.3
  83.3 23.7 %copy-start.4 = (bf16[256,256]{1,0:T(8,128)(2,1)S(1)}, bf16[256,256]{1,0:T(8,128)(2,1)}, u32[]{:S(2)}) copy-start(bf16[256,256]{1,0:T(8,128)(2,1)} %constant.26.clone.second_back) | copy-start | bytes 393220
  83.3 23.7 %copy-start.5 = (bf16[256,256]{1,0:T(8,128)(2,1)S(1)}, bf16[256,256]{1,0:T(8,128)(2,1)}, u32[]{:S(2)}) copy-start(bf16[256,256]{1,0:T(8,128)(2,1)} %constant.25.clone.second) | copy-start | bytes 393220
  83.3 23.7 %copy-start.6 = (f32[64,128]{1,0:T(8,128)S(1)}, f32[64,128]{1,0:T(8,128)}, u32[]{:S(2)}) copy-start(f32[64,128]{1,0:T(8,128)} %constant.24.clone.twist_sin) | copy-start | bytes 98308
  83.4 23.7 %copy-start.7 = (f32[64,128]{1,0:T(8,128)S(1)}, f32[64,128]{1,0:T(8,128)}, u32[]{:S(2)}) copy-start(f32[64,128]{1,0:T(8,128)} %constant.23.clone.twist_cos) | copy-start | bytes 98308
  83.4 23.7 %copy-start.8 = (bf16[128,32]{1,0:T(8,128)(2,1)S(1)}, bf16[128,32]{1,0:T(8,128)(2,1)}, u32[]{:S(2)}) copy-start(bf16[128,32]{1,0:T(8,128)(2,1)} %constant.21.clone.first) | copy-start | bytes 24580
  83.4 23.7 %copy-start.9 = (bf16[32,128]{1,0:T(8,128)(2,1)S(1)}, bf16[32,128]{1,0:T(8,128)(2,1)}, u32[]{:S(2)}) copy-start(bf16[32,128]{1,0:T(8,128)(2,1)} %constant.22.clone.first_back) | copy-start | bytes 24580
  108.3 19.7 %copy-start.1 = (bf16[16,144,256]{2,1,0:T(8,128)(2,1)S(1)}, bf16[16,144,256]{2,1,0:T(8,128)(2,1)}, u32[]{:S(2)}) copy-start(bf16[16,144,256]{2,1,0:T(8,128)(2,1)} %all-gather.3.cloned.1.call-done) | copy-start | bytes 3538948
  127.9 1.8 copy-start.10
  129.8 4.9 %collective-permute-start.2 = (bf16[4,2,2,128,256]{4,3,2,1,0:T(8,128)(2,1)}, bf16[4,2,2,128,256]{4,3,2,1,0:T(8,128)(2,1)}, u32[]{:S(2)}, u32[]{:S(2)}) collective-permute-start(bf16[4,2,2,128,256]{4,3,2,1,0:T(8,128)(2,1)} %get-tuple-element.12), channel_id=1, source_target_pairs={{0,1},{1,0},{2,3},{3,2},{4,5},{5,4},{6,7},{7,6},{8,9},{9,8},{10,11... | collective-permute-start | bytes 3145736 | tf_op jit(solution)/shard_map/ppermute | solution.py:295
  137.2 36.3 %all-to-all-start.3 = ((bf16[8,2,128,256]{3,2,1,0:T(8,128)(2,1)}), bf16[8,2,128,256]{3,2,1,0:T(8,128)(2,1)S(1)}, u32[]{:S(2)}, u32[]{:S(2)}) async-start(bf16[8,2,128,256]{3,2,1,0:T(8,128)(2,1)} %bitcast.11), calls=%async_computation.3 | async-start | bytes 2097152 | tf_op jit(solution)/shard_map/all_to_all | solution.py:297
  173.7 14.9 %collective-permute-start.3 = (bf16[2,128,256]{2,1,0:T(8,128)(2,1)S(1)}, bf16[2,128,256]{2,1,0:T(8,128)(2,1)S(1)}, u32[]{:S(2)}, u32[]{:S(2)}) collective-permute-start(bf16[2,128,256]{2,1,0:T(8,128)(2,1)S(1)} %reduce_sum.12), channel_id=1, source_target_pairs={{0,0},{1,1},{2,2},{3,3},{4,128},{5,129},{6,130},{7,131},{8,256},{9... | collective-permute-start | bytes 393224 | tf_op jit(solution)/shard_map/ppermute | solution.py:301
Sparse Core Ops, SparseCore 0:
  39.1 41.4 all-gather.2
  133.6 37.3 reduce-scatter.1

commit v4 on v3

--- a/solution.py
+++ b/solution.py
@@ -233,9 +233,12 @@
     swap = swap_pairs()
 
     pair, rows = lax.optimization_barrier(
-        (jnp.stack([input_weight, output_weight.T]), jnp.stack([tokens, cotangent]))
-    )
-    weights = lax.all_gather(jnp.pad(pair, ((0, 0), (0, SPARE), (0, 0))), "y", axis=0)
+        (
+            jnp.pad(jnp.stack([input_weight, output_weight.T]), ((0, 0), (0, SPARE), (0, 0))),
+            jnp.stack([tokens, cotangent]),
+        )
+    )
+    weights = lax.all_gather(pair, "y", axis=0)
     moved = lax.ppermute(rows, ALL, swap)
     copies = jnp.broadcast_to(moved[None], (NH * NL, 2, tokens_here, features))
     own = lax.all_to_all(copies, Z, split_axis=0, concat_axis=0, tiled=True)
@@ -248,7 +251,7 @@
         project_own_kernel,
         (me, own, weights),
         jax.ShapeDtypeStruct((2, half, channels), f32),
-        4 * half * 512 * channels,
+        160 * half * 512 * channels,
     )
     sent = call(
         project_kernel,

time: 197 us -> 189 us (0.959)
  blocking collectives: 43.2 us -> 93.9 us
  waiting for transfers between devices: 87 us -> 46.2 us
  starting transfers between devices: 33.2 us -> 16.7 us
  local copies, waits for them, and re-layouts: 8.96 us -> 6.91 us
    all_to_all x0 -> x1, blocking collectives: none -> 41.7 us  [on_device(): own = lax.all_to_all(copies, Z, split_axis=0, concat_axis=0, tiled=True)]
    all_to_all x1 -> x0, waiting for transfers between devices: 28.2 us -> none  [on_device(): own = lax.all_to_all(copies, Z, split_axis=0, concat_axis=0, tiled=True)]
    all_gather x1, waiting for transfers between devices: 13.6 us -> 0.02 us  [on_device(): weights = lax.all_gather(pair, 'y', axis=0)]
    all_to_all x1 -> x0, starting transfers between devices: 13 us -> none  [on_device(): own = lax.all_to_all(copies, Z, split_axis=0, concat_axis=0, tiled=True)]
    all_to_all x1, blocking collectives: 23.6 us -> 28.6 us  [on_device(): lax.all_to_all(sent.reshape(BLOCKS, OWN, 2 * half + 2 * ROWS), CTX, split...]
    all_to_all x1, blocking collectives: 19.6 us -> 23.6 us  [on_device(): got = lax.all_to_all(sent, CTX, split_axis=0, concat_axis=0, tiled=True)]
    all_to_all x1, starting transfers between devices: 7.25 us -> 3.56 us  [on_device(): lax.all_to_all(parts.reshape(NH * NL, 2, tokens_here, features), Z, split...]
  transfers between devices with their start and end apart: 8 -> 7, of which waited for: 6 -> 5; matrix products, arithmetic and copies ran while one was open for 4% -> 3% of each run, Pallas kernels for 1% -> 1%
where the time goes in v4:
time: 189 us
  blocking collectives  93.9 us (50%)
  waiting for transfers between devices  46.2 us (24%)
  starting transfers between devices  16.7 us (9%)
  between operations  14.2 us (8%)
  local copies, waits for them, and re-layouts  6.91 us (4%)
  Pallas kernels  5.76 us (3%)
  other arithmetic  5.04 us (3%)
    all_to_all x1, blocking collectives, on_device(): own = lax.all_to_all(copies, Z, split_axis=0, concat_axis=0, tiled=True)  41.7 us
    all_to_all x1, blocking collectives, on_device(): lax.all_to_all(sent.reshape(BLOCKS, OWN, 2 * half + 2 * ROWS), CTX, split...  28.6 us
    all_to_all x1, waiting for transfers between devices, on_device(): lax.all_to_all(parts.reshape(NH * NL, 2, tokens_here, features), Z, split...  27.7 us
    all_to_all x1, blocking collectives, on_device(): got = lax.all_to_all(sent, CTX, split_axis=0, concat_axis=0, tiled=True)  23.6 us
    ppermute x1, waiting for transfers between devices, on_device(): total = lax.ppermute(total, ALL, swap)  9.33 us
    ppermute x1, waiting for transfers between devices, on_device(): moved = lax.ppermute(rows, ALL, swap)  7 us
    ppermute x1, starting transfers between devices, on_device(): moved = lax.ppermute(rows, ALL, swap)  6.06 us
    pallas_call x5, Pallas kernels, call(): pl.pallas_call(kernel, out_shape=out_shape, in_specs=specs, out_specs=(VM...  5.76 us
  transfers between devices with their start and end apart: 7, of which 5 were waited for; matrix products, arithmetic and copies ran while one was open for 3% of the time, Pallas kernels for 1%

profile of v4, /device:TPU:10, one launch (start us, length us, event | category | flops | bytes accessed | tf_op | source)
XLA Modules:
  0.0 188.8 jit_solution(11030626584572709108)
XLA Ops:
  7.2 0.0 all-gather.3.cloned.1.call-start
  7.2 0.9 copy.21
  8.2 1.5 fusion.2
  9.7 0.9 pad_maximum_fusion
  10.5 0.0 all-gather.3.cloned.1.call-update
  10.6 0.0 reduce-scatter.2.cloned.1.call-start
  10.6 6.1 %collective-permute-start = (bf16[2,128,256]{2,1,0:T(8,128)(2,1)S(1)}, bf16[2,128,256]{2,1,0:T(8,128)(2,1)S(1)}, u32[]{:S(2)}, u32[]{:S(2)}) collective-permute-start(bf16[2,128,256]{2,1,0:T(8,128)(2,1)S(1)} %pad_maximum_fusion), channel_id=1, source_target_pairs={{0,0},{1,1},{2,2},{3,3},{4,128},{5,129},{6,130},{7,131},{8,256},{9... | collective-permute-start | bytes 393224 | tf_op jit(solution)/shard_map/ppermute | solution.py:242
  16.7 7.0 %collective-permute-done = bf16[2,128,256]{2,1,0:T(8,128)(2,1)S(1)} collective-permute-done((bf16[2,128,256]{2,1,0:T(8,128)(2,1)S(1)}, bf16[2,128,256]{2,1,0:T(8,128)(2,1)S(1)}, u32[]{:S(2)}, u32[]{:S(2)}) %collective-permute-start) | collective-permute-done | bytes 131104 | tf_op jit(solution)/shard_map/ppermute | solution.py:242
  23.7 0.1 broadcast_in_dim.2
  23.8 41.7 %all_to_all.20 = bf16[8,2,128,256]{3,2,1,0:T(8,128)(2,1)S(1)} all-to-all(bf16[8,2,128,256]{3,2,1,0:T(8,128)(2,1)S(1)} %broadcast_in_dim.2), channel_id=1, replica_groups=mesh['x'=4,'y'=8,'zh'=4,'zl'=2,'core'=2] {'zh','zl'}, dimensions={0} | all-to-all | bytes 2097152 | tf_op jit(solution)/shard_map/all_to_all | solution.py:244
  65.5 1.9 %collective-permute-start.1 = (bf16[8,2,128,256]{3,2,1,0:T(8,128)(2,1)S(1)}, bf16[8,2,128,256]{3,2,1,0:T(8,128)(2,1)S(1)}, u32[]{:S(2)}, u32[]{:S(2)}) collective-permute-start(bf16[8,2,128,256]{3,2,1,0:T(8,128)(2,1)S(1)} %all_to_all.20), channel_id=1, source_target_pairs={{0,1},{1,0},{2,3},{3,2},{4,5},{5,4},{6,7},{7,6},{8,9},{9,8},{10,11... | collective-permute-start | bytes 3145736 | tf_op jit(solution)/shard_map/ppermute | solution.py:245
  67.4 0.0 all-gather.3.cloned.1.call-done
  67.4 0.0 copy-start
  67.4 1.3 copy-done
  68.7 0.0 copy-start.2
  68.7 0.0 copy-start.3
  68.7 0.4 shard_map.155.totals
  69.1 0.9 collective-permute-done.1
  70.0 0.0 copy-done.2
  70.0 0.0 copy-done.3
  70.0 0.6 shard_map.156
  70.6 0.0 copy-start.4
  70.6 0.0 copy-start.5
  70.6 0.0 copy-start.6
  70.6 0.0 copy-start.7
  70.6 0.0 copy-start.8
  70.7 0.0 copy-start.9
  70.7 28.6 %all_to_all.21.got = bf16[32,8,1280]{2,1,0:T(8,128)(2,1)S(1)} all-to-all(bf16[32,8,1280]{2,1,0:T(8,128)(2,1)S(1)} %bitcast.29), channel_id=1, replica_groups=mesh['x'=4,'y'=8,'zh'=4,'zl'=2,'core'=2] {'x','y'}, dimensions={0} | all-to-all | bytes 1310720 | tf_op jit(solution)/shard_map/all_to_all | solution.py:262
  99.3 0.0 copy-done.4
  99.3 0.0 copy-done.5
  99.3 0.0 copy-done.6
  99.3 0.0 copy-done.7
  99.3 0.0 copy-done.8
  99.3 0.0 copy-done.9
  99.3 1.3 shard_map.157
  100.6 0.0 copy-start.1
  100.6 23.6 %all_to_all.22 = bf16[32,8,1152]{2,1,0:T(8,128)(2,1)S(1)} all-to-all(bf16[32,8,1152]{2,1,0:T(8,128)(2,1)S(1)} %shard_map.157), channel_id=1, replica_groups=mesh['x'=4,'y'=8,'zh'=4,'zl'=2,'core'=2] {'x','y'}, dimensions={0} | all-to-all | bytes 1179648 | tf_op jit(solution)/shard_map/all_to_all | solution.py:281
  124.2 0.0 copy-start.10
  124.2 0.1 slice.24.got
  124.3 0.0 copy-done.1
  124.3 1.7 shard_map.158
  126.0 0.0 copy-done.10
  126.0 1.9 %collective-permute-start.2 = (bf16[4,2,2,128,256]{4,3,2,1,0:T(8,128)(2,1)}, bf16[4,2,2,128,256]{4,3,2,1,0:T(8,128)(2,1)}, u32[]{:S(2)}, u32[]{:S(2)}) collective-permute-start(bf16[4,2,2,128,256]{4,3,2,1,0:T(8,128)(2,1)} %get-tuple-element.12), channel_id=1, source_target_pairs={{0,1},{1,0},{2,3},{3,2},{4,5},{5,4},{6,7},{7,6},{8,9},{9,8},{10,11... | collective-permute-start | bytes 3145736 | tf_op jit(solution)/shard_map/ppermute | solution.py:298
  127.9 1.7 shard_map.159
  129.7 0.0 reduce-scatter.2.cloned.1.call-update
  129.7 1.2 collective-permute-done.2
  130.9 2.5 %add_convert_fusion = bf16[4,2,2,128,256]{4,3,2,1,0:T(8,128)(2,1)} fusion(bf16[4,2,2,128,256]{4,3,2,1,0:T(8,128)(2,1)} %collective-permute-done.2, bf16[4,2,2,128,256]{4,3,2,1,0:T(8,128)(2,1)S(1)} %get-tuple-element.11), kind=kLoop, calls=%fused_computation | loop fusion | flops 2097152 | bytes 3145728 | tf_op jit(solution)/shard_map/convert_element_type | solution.py:299
  133.4 3.6 %all-to-all-start.3 = ((bf16[8,2,128,256]{3,2,1,0:T(8,128)(2,1)}), bf16[8,2,128,256]{3,2,1,0:T(8,128)(2,1)S(1)}, u32[]{:S(2)}, u32[]{:S(2)}) async-start(bf16[8,2,128,256]{3,2,1,0:T(8,128)(2,1)} %bitcast.11), calls=%async_computation.3 | async-start | bytes 2097152 | tf_op jit(solution)/shard_map/all_to_all | solution.py:300
  137.0 0.8 slice_bitcast_fusion.2
  137.8 0.7 copy.22
  138.6 27.7 %all-to-all-done.3 = bf16[8,2,128,256]{3,2,1,0:T(8,128)(2,1)S(1)} async-done(((bf16[8,2,128,256]{3,2,1,0:T(8,128)(2,1)}), bf16[8,2,128,256]{3,2,1,0:T(8,128)(2,1)S(1)}, u32[]{:S(2)}, u32[]{:S(2)}) %all-to-all-start.3) | async-done | bytes 1048608 | tf_op jit(solution)/shard_map/all_to_all | solution.py:300
  166.3 0.1 reduce_sum.12
  166.5 3.2 %collective-permute-start.3 = (bf16[2,128,256]{2,1,0:T(8,128)(2,1)S(1)}, bf16[2,128,256]{2,1,0:T(8,128)(2,1)S(1)}, u32[]{:S(2)}, u32[]{:S(2)}) collective-permute-start(bf16[2,128,256]{2,1,0:T(8,128)(2,1)S(1)} %reduce_sum.12), channel_id=1, source_target_pairs={{0,0},{1,1},{2,2},{3,3},{4,128},{5,129},{6,130},{7,131},{8,256},{9... | collective-permute-start | bytes 393224 | tf_op jit(solution)/shard_map/ppermute | solution.py:304
  169.7 0.0 reduce-scatter.2.cloned.1.call-done
  169.7 1.5 slice_bitcast_fusion
  171.2 0.7 copy.23
  171.9 9.3 %collective-permute-done.3 = bf16[2,128,256]{2,1,0:T(8,128)(2,1)S(1)} collective-permute-done((bf16[2,128,256]{2,1,0:T(8,128)(2,1)S(1)}, bf16[2,128,256]{2,1,0:T(8,128)(2,1)S(1)}, u32[]{:S(2)}, u32[]{:S(2)}) %collective-permute-start.3) | collective-permute-done | bytes 131104 | tf_op jit(solution)/shard_map/ppermute | solution.py:304
  181.3 0.7 slice_bitcast_fusion.3
Async XLA Ops:
  7.2 60.2 %all-gather.3.cloned.1.call-start = ((), (), s32[]{:S(2)}) async-start(), calls=%async_computation.6 | async-start | bytes 1327104 | tf_op jit(solution)/shard_map/all_gather | solution.py:241
  10.6 159.1 %reduce-scatter.2.cloned.1.call-start = ((), (), s32[]{:S(2)}) async-start(), calls=%async_computation.5 | async-start | bytes 1179648 | tf_op jit(solution)/shard_map/reduce_scatter | solution.py:291
  10.6 13.1 %collective-permute-start = (bf16[2,128,256]{2,1,0:T(8,128)(2,1)S(1)}, bf16[2,128,256]{2,1,0:T(8,128)(2,1)S(1)}, u32[]{:S(2)}, u32[]{:S(2)}) collective-permute-start(bf16[2,128,256]{2,1,0:T(8,128)(2,1)S(1)} %pad_maximum_fusion), channel_id=1, source_target_pairs={{0,0},{1,1},{2,2},{3,3},{4,128},{5,129},{6,130},{7,131},{8,256},{9... | collective-permute-start | bytes 393224 | tf_op jit(solution)/shard_map/ppermute | solution.py:242
  65.5 4.5 %collective-permute-start.1 = (bf16[8,2,128,256]{3,2,1,0:T(8,128)(2,1)S(1)}, bf16[8,2,128,256]{3,2,1,0:T(8,128)(2,1)S(1)}, u32[]{:S(2)}, u32[]{:S(2)}) collective-permute-start(bf16[8,2,128,256]{3,2,1,0:T(8,128)(2,1)S(1)} %all_to_all.20), channel_id=1, source_target_pairs={{0,1},{1,0},{2,3},{3,2},{4,5},{5,4},{6,7},{7,6},{8,9},{9,8},{10,11... | collective-permute-start | bytes 3145736 | tf_op jit(solution)/shard_map/ppermute | solution.py:245
  67.4 1.3 copy-start
  68.7 1.3 copy-start.2
  68.7 1.3 copy-start.3
  70.6 28.7 %copy-start.4 = (bf16[256,256]{1,0:T(8,128)(2,1)S(1)}, bf16[256,256]{1,0:T(8,128)(2,1)}, u32[]{:S(2)}) copy-start(bf16[256,256]{1,0:T(8,128)(2,1)} %constant.26.clone.second_back) | copy-start | bytes 393220
  70.6 28.7 %copy-start.5 = (bf16[256,256]{1,0:T(8,128)(2,1)S(1)}, bf16[256,256]{1,0:T(8,128)(2,1)}, u32[]{:S(2)}) copy-start(bf16[256,256]{1,0:T(8,128)(2,1)} %constant.25.clone.second) | copy-start | bytes 393220
  70.6 28.7 %copy-start.6 = (f32[64,128]{1,0:T(8,128)S(1)}, f32[64,128]{1,0:T(8,128)}, u32[]{:S(2)}) copy-start(f32[64,128]{1,0:T(8,128)} %constant.24.clone.twist_sin) | copy-start | bytes 98308
  70.6 28.7 %copy-start.7 = (f32[64,128]{1,0:T(8,128)S(1)}, f32[64,128]{1,0:T(8,128)}, u32[]{:S(2)}) copy-start(f32[64,128]{1,0:T(8,128)} %constant.23.clone.twist_cos) | copy-start | bytes 98308
  70.6 28.7 %copy-start.8 = (bf16[128,32]{1,0:T(8,128)(2,1)S(1)}, bf16[128,32]{1,0:T(8,128)(2,1)}, u32[]{:S(2)}) copy-start(bf16[128,32]{1,0:T(8,128)(2,1)} %constant.21.clone.first) | copy-start | bytes 24580
  70.7 28.7 %copy-start.9 = (bf16[32,128]{1,0:T(8,128)(2,1)S(1)}, bf16[32,128]{1,0:T(8,128)(2,1)}, u32[]{:S(2)}) copy-start(bf16[32,128]{1,0:T(8,128)(2,1)} %constant.22.clone.first_back) | copy-start | bytes 24580
  100.6 23.6 %copy-start.1 = (bf16[16,144,256]{2,1,0:T(8,128)(2,1)S(1)}, bf16[16,144,256]{2,1,0:T(8,128)(2,1)}, u32[]{:S(2)}) copy-start(bf16[16,144,256]{2,1,0:T(8,128)(2,1)} %all-gather.3.cloned.1.call-done) | copy-start | bytes 3538948
  124.2 1.8 copy-start.10
  126.0 4.9 %collective-permute-start.2 = (bf16[4,2,2,128,256]{4,3,2,1,0:T(8,128)(2,1)}, bf16[4,2,2,128,256]{4,3,2,1,0:T(8,128)(2,1)}, u32[]{:S(2)}, u32[]{:S(2)}) collective-permute-start(bf16[4,2,2,128,256]{4,3,2,1,0:T(8,128)(2,1)} %get-tuple-element.12), channel_id=1, source_target_pairs={{0,1},{1,0},{2,3},{3,2},{4,5},{5,4},{6,7},{7,6},{8,9},{9,8},{10,11... | collective-permute-start | bytes 3145736 | tf_op jit(solution)/shard_map/ppermute | solution.py:298
  133.4 32.9 %all-to-all-start.3 = ((bf16[8,2,128,256]{3,2,1,0:T(8,128)(2,1)}), bf16[8,2,128,256]{3,2,1,0:T(8,128)(2,1)S(1)}, u32[]{:S(2)}, u32[]{:S(2)}) async-start(bf16[8,2,128,256]{3,2,1,0:T(8,128)(2,1)} %bitcast.11), calls=%async_computation.3 | async-start | bytes 2097152 | tf_op jit(solution)/shard_map/all_to_all | solution.py:300
  166.5 14.8 %collective-permute-start.3 = (bf16[2,128,256]{2,1,0:T(8,128)(2,1)S(1)}, bf16[2,128,256]{2,1,0:T(8,128)(2,1)S(1)}, u32[]{:S(2)}, u32[]{:S(2)}) collective-permute-start(bf16[2,128,256]{2,1,0:T(8,128)(2,1)S(1)} %reduce_sum.12), channel_id=1, source_target_pairs={{0,0},{1,1},{2,2},{3,3},{4,128},{5,129},{6,130},{7,131},{8,256},{9... | collective-permute-start | bytes 393224 | tf_op jit(solution)/shard_map/ppermute | solution.py:304
Sparse Core Ops, SparseCore 0:
  10.7 45.7 all-gather.2
  129.8 32.4 reduce-scatter.1

commit v5 on v4

--- a/solution.py
+++ b/solution.py
@@ -21,7 +21,7 @@
 ROWS = 128
 FREQS = 2 * BLOCKS
 LENGTH = FREQS * ROWS
-SPARE = 16
+SPARE = 8
 OWN = 8
 
 VMEM = pl.BlockSpec(memory_space=pltpu.VMEM)
@@ -232,14 +232,9 @@
     me = lax.axis_index("core").astype(jnp.int32).reshape(1)
     swap = swap_pairs()
 
-    pair, rows = lax.optimization_barrier(
-        (
-            jnp.pad(jnp.stack([input_weight, output_weight.T]), ((0, 0), (0, SPARE), (0, 0))),
-            jnp.stack([tokens, cotangent]),
-        )
-    )
+    pair = jnp.pad(jnp.stack([input_weight, output_weight.T]), ((0, 0), (0, SPARE), (0, 0)))
     weights = lax.all_gather(pair, "y", axis=0)
-    moved = lax.ppermute(rows, ALL, swap)
+    moved = lax.ppermute(jnp.stack([tokens, cotangent]), ALL, swap)
     copies = jnp.broadcast_to(moved[None], (NH * NL, 2, tokens_here, features))
     own = lax.all_to_all(copies, Z, split_axis=0, concat_axis=0, tiled=True)
     other = lax.ppermute(own, "core", [(0, 1), (1, 0)])

time: 189 us -> 187 us (0.989)
  waiting for transfers between devices: 46.2 us -> 43.7 us
    ppermute x1, waiting for transfers between devices: 7 us -> 4.47 us  [on_device(): moved = lax.ppermute(jnp.stack([tokens, cotangent]), ALL, swap)]
  transfers between devices with their start and end apart: 7 -> 7, of which waited for: 5 -> 5; matrix products, arithmetic and copies ran while one was open for 3% -> 5% of each run, Pallas kernels for 1% -> 1%
where the time goes in v5:
time: 187 us; the launch traced here: 186 us
  blocking collectives  93.9 us (50%)
  waiting for transfers between devices  43.7 us (23%)
  starting transfers between devices  16.7 us (9%)
  between operations  14.3 us (8%)
  local copies, waits for them, and re-layouts  6.88 us (4%)
  Pallas kernels  5.77 us (3%)
  other arithmetic  5.07 us (3%)
    all_to_all x1, blocking collectives, on_device(): own = lax.all_to_all(copies, Z, split_axis=0, concat_axis=0, tiled=True)  41.7 us
    all_to_all x1, blocking collectives, on_device(): lax.all_to_all(sent.reshape(BLOCKS, OWN, 2 * half + 2 * ROWS), CTX, split...  28.6 us
    all_to_all x1, waiting for transfers between devices, on_device(): lax.all_to_all(parts.reshape(NH * NL, 2, tokens_here, features), Z, split...  27.7 us
    all_to_all x1, blocking collectives, on_device(): got = lax.all_to_all(sent, CTX, split_axis=0, concat_axis=0, tiled=True)  23.6 us
    ppermute x1, waiting for transfers between devices, on_device(): total = lax.ppermute(total, ALL, swap)  9.33 us
    ppermute x1, starting transfers between devices, on_device(): moved = lax.ppermute(jnp.stack([tokens, cotangent]), ALL, swap)  6.06 us
    pallas_call x5, Pallas kernels, call(): pl.pallas_call(kernel, out_shape=out_shape, in_specs=specs, out_specs=(VM...  5.77 us
    ppermute x1, waiting for transfers between devices, on_device(): moved = lax.ppermute(jnp.stack([tokens, cotangent]), ALL, swap)  4.47 us
  transfers between devices with their start and end apart: 7, of which 5 were waited for; matrix products, arithmetic and copies ran while one was open for 5% of the time, Pallas kernels for 1%

profile of v5, /device:TPU:10, one launch (start us, length us, event | category | flops | bytes accessed | tf_op | source)
XLA Modules:
  0.0 186.3 jit_solution(7487662186686524092)
XLA Ops:
  7.2 0.0 all-gather.3.cloned.1.call-start
  7.2 0.9 pad_maximum_fusion
  8.1 6.1 %collective-permute-start = (bf16[2,128,256]{2,1,0:T(8,128)(2,1)S(1)}, bf16[2,128,256]{2,1,0:T(8,128)(2,1)S(1)}, u32[]{:S(2)}, u32[]{:S(2)}) collective-permute-start(bf16[2,128,256]{2,1,0:T(8,128)(2,1)S(1)} %pad_maximum_fusion), channel_id=1, source_target_pairs={{0,0},{1,1},{2,2},{3,3},{4,128},{5,129},{6,130},{7,131},{8,256},{9... | collective-permute-start | bytes 393224 | tf_op jit(solution)/shard_map/ppermute | solution.py:237
  14.2 0.9 copy.21
  15.1 1.5 fusion.2
  16.6 0.0 all-gather.3.cloned.1.call-update
  16.7 0.0 reduce-scatter.2.cloned.1.call-start
  16.7 4.5 %collective-permute-done = bf16[2,128,256]{2,1,0:T(8,128)(2,1)S(1)} collective-permute-done((bf16[2,128,256]{2,1,0:T(8,128)(2,1)S(1)}, bf16[2,128,256]{2,1,0:T(8,128)(2,1)S(1)}, u32[]{:S(2)}, u32[]{:S(2)}) %collective-permute-start) | collective-permute-done | bytes 131104 | tf_op jit(solution)/shard_map/ppermute | solution.py:237
  21.2 0.1 broadcast_in_dim.2
  21.3 41.7 %all_to_all.20 = bf16[8,2,128,256]{3,2,1,0:T(8,128)(2,1)S(1)} all-to-all(bf16[8,2,128,256]{3,2,1,0:T(8,128)(2,1)S(1)} %broadcast_in_dim.2), channel_id=1, replica_groups=mesh['x'=4,'y'=8,'zh'=4,'zl'=2,'core'=2] {'zh','zl'}, dimensions={0} | all-to-all | bytes 2097152 | tf_op jit(solution)/shard_map/all_to_all | solution.py:239
  63.0 1.9 %collective-permute-start.1 = (bf16[8,2,128,256]{3,2,1,0:T(8,128)(2,1)S(1)}, bf16[8,2,128,256]{3,2,1,0:T(8,128)(2,1)S(1)}, u32[]{:S(2)}, u32[]{:S(2)}) collective-permute-start(bf16[8,2,128,256]{3,2,1,0:T(8,128)(2,1)S(1)} %all_to_all.20), channel_id=1, source_target_pairs={{0,1},{1,0},{2,3},{3,2},{4,5},{5,4},{6,7},{7,6},{8,9},{9,8},{10,11... | collective-permute-start | bytes 3145736 | tf_op jit(solution)/shard_map/ppermute | solution.py:240
  64.9 0.0 all-gather.3.cloned.1.call-done
  64.9 0.0 copy-start
  64.9 1.2 copy-done
  66.2 0.0 copy-start.2
  66.2 0.0 copy-start.3
  66.2 0.4 shard_map.155.totals
  66.6 0.9 collective-permute-done.1
  67.5 0.0 copy-done.2
  67.5 0.0 copy-done.3
  67.5 0.6 shard_map.156
  68.1 0.0 copy-start.4
  68.1 0.0 copy-start.5
  68.1 0.0 copy-start.6
  68.1 0.0 copy-start.7
  68.1 0.0 copy-start.8
  68.1 0.0 copy-start.9
  68.2 28.6 %all_to_all.21.got = bf16[32,8,1280]{2,1,0:T(8,128)(2,1)S(1)} all-to-all(bf16[32,8,1280]{2,1,0:T(8,128)(2,1)S(1)} %bitcast.29), channel_id=1, replica_groups=mesh['x'=4,'y'=8,'zh'=4,'zl'=2,'core'=2] {'x','y'}, dimensions={0} | all-to-all | bytes 1310720 | tf_op jit(solution)/shard_map/all_to_all | solution.py:257
  96.8 0.0 copy-done.4
  96.8 0.0 copy-done.5
  96.8 0.0 copy-done.6
  96.8 0.0 copy-done.7
  96.8 0.0 copy-done.8
  96.8 0.0 copy-done.9
  96.8 1.3 shard_map.157
  98.1 0.0 copy-start.1
  98.1 23.6 %all_to_all.22 = bf16[32,8,1152]{2,1,0:T(8,128)(2,1)S(1)} all-to-all(bf16[32,8,1152]{2,1,0:T(8,128)(2,1)S(1)} %shard_map.157), channel_id=1, replica_groups=mesh['x'=4,'y'=8,'zh'=4,'zl'=2,'core'=2] {'x','y'}, dimensions={0} | all-to-all | bytes 1179648 | tf_op jit(solution)/shard_map/all_to_all | solution.py:276
  121.7 0.0 copy-start.10
  121.7 0.1 slice.24.got
  121.8 0.0 copy-done.1
  121.8 1.7 shard_map.158
  123.5 0.0 copy-done.10
  123.5 1.9 %collective-permute-start.2 = (bf16[4,2,2,128,256]{4,3,2,1,0:T(8,128)(2,1)}, bf16[4,2,2,128,256]{4,3,2,1,0:T(8,128)(2,1)}, u32[]{:S(2)}, u32[]{:S(2)}) collective-permute-start(bf16[4,2,2,128,256]{4,3,2,1,0:T(8,128)(2,1)} %get-tuple-element.8), channel_id=1, source_target_pairs={{0,1},{1,0},{2,3},{3,2},{4,5},{5,4},{6,7},{7,6},{8,9},{9,8},{10,11... | collective-permute-start | bytes 3145736 | tf_op jit(solution)/shard_map/ppermute | solution.py:293
  125.4 1.7 shard_map.159
  127.1 0.0 reduce-scatter.2.cloned.1.call-update
  127.2 1.2 collective-permute-done.2
  128.4 2.5 %add_convert_fusion = bf16[4,2,2,128,256]{4,3,2,1,0:T(8,128)(2,1)} fusion(bf16[4,2,2,128,256]{4,3,2,1,0:T(8,128)(2,1)} %collective-permute-done.2, bf16[4,2,2,128,256]{4,3,2,1,0:T(8,128)(2,1)S(1)} %get-tuple-element.7), kind=kLoop, calls=%fused_computation | loop fusion | flops 2097152 | bytes 3145728 | tf_op jit(solution)/shard_map/convert_element_type | solution.py:294
  130.9 3.6 %all-to-all-start.3 = ((bf16[8,2,128,256]{3,2,1,0:T(8,128)(2,1)}), bf16[8,2,128,256]{3,2,1,0:T(8,128)(2,1)S(1)}, u32[]{:S(2)}, u32[]{:S(2)}) async-start(bf16[8,2,128,256]{3,2,1,0:T(8,128)(2,1)} %bitcast.11), calls=%async_computation.3 | async-start | bytes 2097152 | tf_op jit(solution)/shard_map/all_to_all | solution.py:295
  134.5 0.8 slice_bitcast_fusion.2
  135.3 0.7 copy.22
  136.1 27.7 %all-to-all-done.3 = bf16[8,2,128,256]{3,2,1,0:T(8,128)(2,1)S(1)} async-done(((bf16[8,2,128,256]{3,2,1,0:T(8,128)(2,1)}), bf16[8,2,128,256]{3,2,1,0:T(8,128)(2,1)S(1)}, u32[]{:S(2)}, u32[]{:S(2)}) %all-to-all-start.3) | async-done | bytes 1048608 | tf_op jit(solution)/shard_map/all_to_all | solution.py:295
  163.8 0.1 reduce_sum.12
  163.9 3.2 %collective-permute-start.3 = (bf16[2,128,256]{2,1,0:T(8,128)(2,1)S(1)}, bf16[2,128,256]{2,1,0:T(8,128)(2,1)S(1)}, u32[]{:S(2)}, u32[]{:S(2)}) collective-permute-start(bf16[2,128,256]{2,1,0:T(8,128)(2,1)S(1)} %reduce_sum.12), channel_id=1, source_target_pairs={{0,0},{1,1},{2,2},{3,3},{4,128},{5,129},{6,130},{7,131},{8,256},{9... | collective-permute-start | bytes 393224 | tf_op jit(solution)/shard_map/ppermute | solution.py:299
  167.1 0.0 reduce-scatter.2.cloned.1.call-done
  167.2 1.5 slice_bitcast_fusion
  168.7 0.7 copy.23
  169.4 9.3 %collective-permute-done.3 = bf16[2,128,256]{2,1,0:T(8,128)(2,1)S(1)} collective-permute-done((bf16[2,128,256]{2,1,0:T(8,128)(2,1)S(1)}, bf16[2,128,256]{2,1,0:T(8,128)(2,1)S(1)}, u32[]{:S(2)}, u32[]{:S(2)}) %collective-permute-start.3) | collective-permute-done | bytes 131104 | tf_op jit(solution)/shard_map/ppermute | solution.py:299
  178.8 0.7 slice_bitcast_fusion.3
Async XLA Ops:
  7.2 57.7 %all-gather.3.cloned.1.call-start = ((), (), s32[]{:S(2)}) async-start(), calls=%async_computation.6 | async-start | bytes 1253376 | tf_op jit(solution)/shard_map/all_gather | solution.py:236
  8.1 13.1 %collective-permute-start = (bf16[2,128,256]{2,1,0:T(8,128)(2,1)S(1)}, bf16[2,128,256]{2,1,0:T(8,128)(2,1)S(1)}, u32[]{:S(2)}, u32[]{:S(2)}) collective-permute-start(bf16[2,128,256]{2,1,0:T(8,128)(2,1)S(1)} %pad_maximum_fusion), channel_id=1, source_target_pairs={{0,0},{1,1},{2,2},{3,3},{4,128},{5,129},{6,130},{7,131},{8,256},{9... | collective-permute-start | bytes 393224 | tf_op jit(solution)/shard_map/ppermute | solution.py:237
  16.7 150.5 %reduce-scatter.2.cloned.1.call-start = ((), (), s32[]{:S(2)}) async-start(), calls=%async_computation.5 | async-start | bytes 1179648 | tf_op jit(solution)/shard_map/reduce_scatter | solution.py:286
  63.0 4.5 %collective-permute-start.1 = (bf16[8,2,128,256]{3,2,1,0:T(8,128)(2,1)S(1)}, bf16[8,2,128,256]{3,2,1,0:T(8,128)(2,1)S(1)}, u32[]{:S(2)}, u32[]{:S(2)}) collective-permute-start(bf16[8,2,128,256]{3,2,1,0:T(8,128)(2,1)S(1)} %all_to_all.20), channel_id=1, source_target_pairs={{0,1},{1,0},{2,3},{3,2},{4,5},{5,4},{6,7},{7,6},{8,9},{9,8},{10,11... | collective-permute-start | bytes 3145736 | tf_op jit(solution)/shard_map/ppermute | solution.py:240
  64.9 1.2 copy-start
  66.2 1.3 copy-start.2
  66.2 1.3 copy-start.3
  68.1 28.7 %copy-start.4 = (bf16[256,256]{1,0:T(8,128)(2,1)S(1)}, bf16[256,256]{1,0:T(8,128)(2,1)}, u32[]{:S(2)}) copy-start(bf16[256,256]{1,0:T(8,128)(2,1)} %constant.26.clone.second_back) | copy-start | bytes 393220
  68.1 28.7 %copy-start.5 = (bf16[256,256]{1,0:T(8,128)(2,1)S(1)}, bf16[256,256]{1,0:T(8,128)(2,1)}, u32[]{:S(2)}) copy-start(bf16[256,256]{1,0:T(8,128)(2,1)} %constant.25.clone.second) | copy-start | bytes 393220
  68.1 28.7 %copy-start.6 = (f32[64,128]{1,0:T(8,128)S(1)}, f32[64,128]{1,0:T(8,128)}, u32[]{:S(2)}) copy-start(f32[64,128]{1,0:T(8,128)} %constant.24.clone.twist_sin) | copy-start | bytes 98308
  68.1 28.7 %copy-start.7 = (f32[64,128]{1,0:T(8,128)S(1)}, f32[64,128]{1,0:T(8,128)}, u32[]{:S(2)}) copy-start(f32[64,128]{1,0:T(8,128)} %constant.23.clone.twist_cos) | copy-start | bytes 98308
  68.1 28.7 %copy-start.8 = (bf16[128,32]{1,0:T(8,128)(2,1)S(1)}, bf16[128,32]{1,0:T(8,128)(2,1)}, u32[]{:S(2)}) copy-start(bf16[128,32]{1,0:T(8,128)(2,1)} %constant.21.clone.first) | copy-start | bytes 24580
  68.1 28.7 %copy-start.9 = (bf16[32,128]{1,0:T(8,128)(2,1)S(1)}, bf16[32,128]{1,0:T(8,128)(2,1)}, u32[]{:S(2)}) copy-start(bf16[32,128]{1,0:T(8,128)(2,1)} %constant.22.clone.first_back) | copy-start | bytes 24580
  98.1 23.6 %copy-start.1 = (bf16[16,136,256]{2,1,0:T(8,128)(2,1)S(1)}, bf16[16,136,256]{2,1,0:T(8,128)(2,1)}, u32[]{:S(2)}) copy-start(bf16[16,136,256]{2,1,0:T(8,128)(2,1)} %all-gather.3.cloned.1.call-done) | copy-start | bytes 3342340
  121.7 1.8 copy-start.10
  123.5 4.9 %collective-permute-start.2 = (bf16[4,2,2,128,256]{4,3,2,1,0:T(8,128)(2,1)}, bf16[4,2,2,128,256]{4,3,2,1,0:T(8,128)(2,1)}, u32[]{:S(2)}, u32[]{:S(2)}) collective-permute-start(bf16[4,2,2,128,256]{4,3,2,1,0:T(8,128)(2,1)} %get-tuple-element.8), channel_id=1, source_target_pairs={{0,1},{1,0},{2,3},{3,2},{4,5},{5,4},{6,7},{7,6},{8,9},{9,8},{10,11... | collective-permute-start | bytes 3145736 | tf_op jit(solution)/shard_map/ppermute | solution.py:293
  130.9 32.9 %all-to-all-start.3 = ((bf16[8,2,128,256]{3,2,1,0:T(8,128)(2,1)}), bf16[8,2,128,256]{3,2,1,0:T(8,128)(2,1)S(1)}, u32[]{:S(2)}, u32[]{:S(2)}) async-start(bf16[8,2,128,256]{3,2,1,0:T(8,128)(2,1)} %bitcast.11), calls=%async_computation.3 | async-start | bytes 2097152 | tf_op jit(solution)/shard_map/all_to_all | solution.py:295
  163.9 14.8 %collective-permute-start.3 = (bf16[2,128,256]{2,1,0:T(8,128)(2,1)S(1)}, bf16[2,128,256]{2,1,0:T(8,128)(2,1)S(1)}, u32[]{:S(2)}, u32[]{:S(2)}) collective-permute-start(bf16[2,128,256]{2,1,0:T(8,128)(2,1)S(1)} %reduce_sum.12), channel_id=1, source_target_pairs={{0,0},{1,1},{2,2},{3,3},{4,128},{5,129},{6,130},{7,131},{8,256},{9... | collective-permute-start | bytes 393224 | tf_op jit(solution)/shard_map/ppermute | solution.py:299
Sparse Core Ops, SparseCore 0:
  16.8 45.0 all-gather.2
  127.3 32.4 reduce-scatter.1

commit v6 on v5

--- a/solution.py
+++ b/solution.py
@@ -86,7 +86,11 @@
         totals[which] = product_terms(own, weights, which, me_ref[0])
 
 
-def project_kernel(me_ref, other, weights, totals, filters, gate, out):
+def project_kernel(me_ref, other, weights, totals, filters, gate, out, half_out):
+    first = 2 * (1 - me_ref[0])
+    for l in range(NL):
+        for i in range(2):
+            half_out[l, i] = weights[4 * l + first + i, :, :ROWS]
     for which in range(2):
         total = totals[which] + product_terms(other, weights, which, 1 - me_ref[0])
         out[:, which * NX * ROWS : (which + 1) * NX * ROWS] = total.T.astype(bf16)
@@ -191,19 +195,21 @@
                 out[4 * l + 2 * c + 1, which] = total[:, ROWS:]
 
 
-def output_kernel(me_ref, got, weights, keep, send):
-    me = me_ref[0]
+def output_kernel(me_ref, got, got_other, weights, weights_other, out):
     half = NX * ROWS
     for which in range(2):
-        start = which * half
-        rows = got[:, start : start + half].astype(f32).T.astype(bf16)
+        lanes = slice(which * half, (which + 1) * half)
+        rows = [held[:, lanes].astype(f32).T.astype(bf16) for held in (got, got_other)]
         for l in range(NL):
-            for held, c in ((keep, me), (send, 1 - me)):
-                block = weight_block(weights, 1 - which, l, c)
-                total = lax.dot_general(
-                    rows, block, (((1,), (1,)), ((), ())), preferred_element_type=f32
+            other = [weights_other[l, i, 1 - which] for i in range(2)]
+            blocks = (weight_block(weights, 1 - which, l, me_ref[0]), jnp.concatenate(other, 0))
+            total = None
+            for left, right in zip(rows, blocks):
+                term = lax.dot_general(
+                    left, right, (((1,), (1,)), ((), ())), preferred_element_type=f32
                 )
-                held[:, l, which] = total.astype(bf16).reshape(NX, ROWS, 2 * ROWS)
+                total = term if total is None else total + term
+            out[:, l, which] = total.astype(bf16).reshape(NX, ROWS, 2 * ROWS)
 
 
 def call(kernel, inputs, out_shape, flops, scratch=(), first_smem=True):
@@ -248,12 +254,16 @@
         jax.ShapeDtypeStruct((2, half, channels), f32),
         160 * half * 512 * channels,
     )
-    sent = call(
+    sent, weights_half = call(
         project_kernel,
         (me, other, weights, totals, filters, gate_values),
-        jax.ShapeDtypeStruct((channels, 2 * half + 2 * ROWS), bf16),
+        (
+            jax.ShapeDtypeStruct((channels, 2 * half + 2 * ROWS), bf16),
+            jax.ShapeDtypeStruct((NL, 2, 2, ROWS, channels), bf16),
+        ),
         4 * half * 512 * channels,
     )
+    weights_other = lax.ppermute(weights_half, "core", [(0, 1), (1, 0)])
     got = lax.all_to_all(
         sent.reshape(BLOCKS, OWN, 2 * half + 2 * ROWS), CTX, split_axis=0, concat_axis=0, tiled=True
     )
@@ -286,12 +296,13 @@
     grads = lax.psum_scatter(grads, "y", scatter_dimension=0, tiled=True)
     grad_input_weight, grad_output_weight = grads[0, 0].T, grads[0, 1]
 
-    shape = jax.ShapeDtypeStruct(held, bf16)
-    keep, send = call(
-        output_kernel, (me, streams, weights), (shape, shape), 4 * half * 1024 * channels
-    )
-    arrived = lax.ppermute(send, "core", [(0, 1), (1, 0)])
-    parts = (keep.astype(f32) + arrived.astype(f32)).astype(bf16)
+    streams_other = lax.ppermute(streams, "core", [(0, 1), (1, 0)])
+    parts = call(
+        output_kernel,
+        (me, streams, streams_other, weights, weights_other),
+        jax.ShapeDtypeStruct(held, bf16),
+        4 * half * 1024 * channels,
+    )
     parts = lax.all_to_all(
         parts.reshape(NH * NL, 2, tokens_here, features), Z, split_axis=0, concat_axis=0, tiled=True
     )

time: 187 us -> 190 us (1.016)
  blocking collectives: 93.9 us -> 70.4 us
  waiting for transfers between devices: 43.7 us -> 58.8 us
  starting transfers between devices: 16.7 us -> 24.6 us
  Pallas kernels: 5.77 us -> 9.86 us
  other arithmetic: 5.07 us -> 2.53 us
  local copies, waits for them, and re-layouts: 6.88 us -> 8.9 us
    all_to_all x1 -> x0, blocking collectives: 23.6 us -> none  [on_device(): got = lax.all_to_all(sent, CTX, split_axis=0, concat_axis=0, tiled=True)]
    all_to_all x0 -> x1, waiting for transfers between devices: none -> 15.9 us  [on_device(): got = lax.all_to_all(sent, CTX, split_axis=0, concat_axis=0, tiled=True)]
    all_to_all x0 -> x1, starting transfers between devices: none -> 5.87 us  [on_device(): got = lax.all_to_all(sent, CTX, split_axis=0, concat_axis=0, tiled=True)]
    pallas_call x5, Pallas kernels: 5.77 us -> 9.86 us  [call(): pl.pallas_call(kernel, out_shape=out_shape, in_specs=specs, out_specs=(VM...]
    convert_element_type x1 -> x0, other arithmetic: 2.52 us -> none  [on_device(): parts = (keep.astype(f32) + arrived.astype(f32)).astype(bf16)]
    ppermute x1 -> x2, starting transfers between devices: 1.91 us -> 3.84 us  [the longest x1 1.92 us: on_device(): streams_other = lax.ppermute(streams, 'core', [(0, 1), (1, 0)])]
  transfers between devices with their start and end apart: 7 -> 9, of which waited for: 5 -> 5; matrix products, arithmetic and copies ran while one was open for 5% -> 4% of each run, Pallas kernels for 1% -> 3%
where the time goes in v6:
time: 190 us; the launch traced here: 189 us
  blocking collectives  70.4 us (37%)
  waiting for transfers between devices  58.8 us (31%)
  starting transfers between devices  24.6 us (13%)
  between operations  14.2 us (7%)
  Pallas kernels  9.86 us (5%)
  local copies, waits for them, and re-layouts  8.9 us (5%)
  other arithmetic  2.53 us (1%)
    all_to_all x1, blocking collectives, on_device(): own = lax.all_to_all(copies, Z, split_axis=0, concat_axis=0, tiled=True)  41.7 us
    all_to_all x1, blocking collectives, on_device(): lax.all_to_all(sent.reshape(BLOCKS, OWN, 2 * half + 2 * ROWS), CTX, split...  28.8 us
    all_to_all x1, waiting for transfers between devices, on_device(): lax.all_to_all(parts.reshape(NH * NL, 2, tokens_here, features), Z, split...  28 us
    all_to_all x1, waiting for transfers between devices, on_device(): got = lax.all_to_all(sent, CTX, split_axis=0, concat_axis=0, tiled=True)  15.9 us
    pallas_call x5, Pallas kernels, call(): pl.pallas_call(kernel, out_shape=out_shape, in_specs=specs, out_specs=(VM...  9.86 us
    ppermute x1, waiting for transfers between devices, on_device(): total = lax.ppermute(total, ALL, swap)  9.26 us
    ppermute x1, starting transfers between devices, on_device(): moved = lax.ppermute(jnp.stack([tokens, cotangent]), ALL, swap)  6.06 us
    all_to_all x1, starting transfers between devices, on_device(): got = lax.all_to_all(sent, CTX, split_axis=0, concat_axis=0, tiled=True)  5.87 us
  transfers between devices with their start and end apart: 9, of which 5 were waited for; matrix products, arithmetic and copies ran while one was open for 4% of the time, Pallas kernels for 3%

profile of v6, /device:TPU:10, one launch (start us, length us, event | category | flops | bytes accessed | tf_op | source)
XLA Modules:
  0.0 189.4 jit_solution(42207568907987844)
XLA Ops:
  7.2 0.0 all-gather.3.cloned.1.call-start
  7.2 0.9 pad_maximum_fusion
  8.1 6.1 %collective-permute-start = (bf16[2,128,256]{2,1,0:T(8,128)(2,1)S(1)}, bf16[2,128,256]{2,1,0:T(8,128)(2,1)S(1)}, u32[]{:S(2)}, u32[]{:S(2)}) collective-permute-start(bf16[2,128,256]{2,1,0:T(8,128)(2,1)S(1)} %pad_maximum_fusion), channel_id=1, source_target_pairs={{0,0},{1,1},{2,2},{3,3},{4,128},{5,129},{6,130},{7,131},{8,256},{9... | collective-permute-start | bytes 393224 | tf_op jit(solution)/shard_map/ppermute | solution.py:243
  14.2 0.9 copy.21
  15.1 1.5 fusion.2
  16.6 0.0 all-gather.3.cloned.1.call-update
  16.6 4.5 %collective-permute-done = bf16[2,128,256]{2,1,0:T(8,128)(2,1)S(1)} collective-permute-done((bf16[2,128,256]{2,1,0:T(8,128)(2,1)S(1)}, bf16[2,128,256]{2,1,0:T(8,128)(2,1)S(1)}, u32[]{:S(2)}, u32[]{:S(2)}) %collective-permute-start) | collective-permute-done | bytes 131104 | tf_op jit(solution)/shard_map/ppermute | solution.py:243
  21.2 0.1 broadcast_in_dim.2
  21.3 41.7 %all_to_all.20 = bf16[8,2,128,256]{3,2,1,0:T(8,128)(2,1)S(1)} all-to-all(bf16[8,2,128,256]{3,2,1,0:T(8,128)(2,1)S(1)} %broadcast_in_dim.2), channel_id=1, replica_groups=mesh['x'=4,'y'=8,'zh'=4,'zl'=2,'core'=2] {'zh','zl'}, dimensions={0} | all-to-all | bytes 2097152 | tf_op jit(solution)/shard_map/all_to_all | solution.py:245
  63.0 1.9 %collective-permute-start.1 = (bf16[8,2,128,256]{3,2,1,0:T(8,128)(2,1)S(1)}, bf16[8,2,128,256]{3,2,1,0:T(8,128)(2,1)}, u32[]{:S(2)}, u32[]{:S(2)}) collective-permute-start(bf16[8,2,128,256]{3,2,1,0:T(8,128)(2,1)S(1)} %all_to_all.20), channel_id=1, source_target_pairs={{0,1},{1,0},{2,3},{3,2},{4,5},{5,4},{6,7},{7,6},{8,9},{9,8},{10,11... | collective-permute-start | bytes 3145736 | tf_op jit(solution)/shard_map/ppermute | solution.py:246
  64.9 0.0 all-gather.3.cloned.1.call-done
  64.9 0.0 copy-start
  64.9 1.2 copy-done
  66.2 0.0 copy-start.1
  66.2 0.0 copy-start.3
  66.2 0.0 copy-start.4
  66.2 0.4 shard_map.155.totals
  66.6 1.0 collective-permute-done.1
  67.6 0.0 copy-done.1
  67.6 0.0 copy-done.3
  67.6 0.0 copy-done.4
  67.6 2.6 %shard_map.156 = (bf16[256,1280]{1,0:T(8,128)(2,1)S(1)}, bf16[2,2,2,128,256]{4,3,2,1,0:T(8,128)(2,1)}) custom-call(s32[1]{0:T(128)} %bitcast.me_ref, bf16[4,2,2,128,256]{4,3,2,1,0:T(8,128)(2,1)} %bitcast.3.other, bf16[8,2,136,256]{3,2,1,0:T(8,128)(2,1)S(1)} %bitcast.26, f32[2,512,256]{2,1,0:T(8,128)S(1)} %shard_map.155.totals, ...), custom_call_target="tpu_custom_call" | custom-call | flops 268435456 | bytes 3342340 | tf_op jit(solution)/shard_map/pallas_call | solution.py:220
  70.2 0.0 copy-start.5
  70.2 0.0 copy-start.6
  70.2 0.0 copy-start.7
  70.2 0.0 copy-start.8
  70.2 0.0 copy-start.9
  70.2 0.0 copy-start.10
  70.2 28.8 %all_to_all.21.got = bf16[32,8,1280]{2,1,0:T(8,128)(2,1)S(1)} all-to-all(bf16[32,8,1280]{2,1,0:T(8,128)(2,1)S(1)} %bitcast.30), channel_id=1, replica_groups=mesh['x'=4,'y'=8,'zh'=4,'zl'=2,'core'=2] {'x','y'}, dimensions={0} | all-to-all | bytes 1310720 | tf_op jit(solution)/shard_map/all_to_all | solution.py:267
  99.0 0.0 copy-done.5
  99.0 0.0 copy-done.6
  99.0 0.0 copy-done.7
  99.0 0.0 copy-done.8
  99.0 0.0 copy-done.9
  99.0 0.0 copy-done.10
  99.0 2.1 %shard_map.157 = bf16[32,8,1152]{2,1,0:T(8,128)(2,1)} custom-call(bf16[32,8,1280]{2,1,0:T(8,128)(2,1)S(1)} %all_to_all.21.got, bf16[128,32]{1,0:T(8,128)(2,1)S(1)} %copy-done.9, bf16[32,128]{1,0:T(8,128)(2,1)S(1)} %copy-done.10, f32[64,128]{1,0:T(8,128)S(1)} %copy-done.8, f32[64,128]{1,0:T(8,128)S(1)} %copy-done.7, bf16[256,256]{1,0:T(8,128)(2,1)S(1)} %copy-done.6, ...), custom_call_target="tpu_custom_call" | custom-call | flops 2684354560 | bytes 999424 | tf_op jit(solution)/shard_map/pallas_call | solution.py:220
  101.2 5.9 %all-to-all-start.2 = ((bf16[32,8,1152]{2,1,0:T(8,128)(2,1)}), bf16[32,8,1152]{2,1,0:T(8,128)(2,1)}, u32[]{:S(2)}, u32[]{:S(2)}) async-start(bf16[32,8,1152]{2,1,0:T(8,128)(2,1)} %shard_map.157), calls=%async_computation.2 | async-start | bytes 1179648 | tf_op jit(solution)/shard_map/all_to_all | solution.py:286
  107.0 0.0 reduce-scatter.2.cloned.1.call-start
  107.1 1.9 %collective-permute-start.3 = (bf16[2,2,2,128,256]{4,3,2,1,0:T(8,128)(2,1)}, bf16[2,2,2,128,256]{4,3,2,1,0:T(8,128)(2,1)S(1)}, u32[]{:S(2)}, u32[]{:S(2)}) collective-permute-start(bf16[2,2,2,128,256]{4,3,2,1,0:T(8,128)(2,1)} %get-tuple-element.8), channel_id=1, source_target_pairs={{0,1},{1,0},{2,3},{3,2},{4,5},{5,4},{6,7},{7,6},{8,9},{9,8},{10,11... | collective-permute-start | bytes 1572872 | tf_op jit(solution)/shard_map/ppermute | solution.py:266
  109.0 15.9 %all-to-all-done.2 = bf16[32,8,1152]{2,1,0:T(8,128)(2,1)} async-done(((bf16[32,8,1152]{2,1,0:T(8,128)(2,1)}), bf16[32,8,1152]{2,1,0:T(8,128)(2,1)}, u32[]{:S(2)}, u32[]{:S(2)}) %all-to-all-start.2) | async-done | bytes 589856 | tf_op jit(solution)/shard_map/all_to_all | solution.py:286
  124.9 1.1 slice.24.got
  126.0 1.9 %collective-permute-start.2 = (bf16[256,1024]{1,0:T(8,128)(2,1)S(1)}, bf16[256,1024]{1,0:T(8,128)(2,1)}, u32[]{:S(2)}, u32[]{:S(2)}) collective-permute-start(bf16[256,1024]{1,0:T(8,128)(2,1)S(1)} %slice.24.got), channel_id=1, source_target_pairs={{0,1},{1,0},{2,3},{3,2},{4,5},{5,4},{6,7},{7,6},{8,9},{9,8},{10,11... | collective-permute-start | bytes 1572872 | tf_op jit(solution)/shard_map/ppermute | solution.py:299
  127.9 1.9 %shard_map.159 = bf16[8,2,256,128]{3,2,1,0:T(8,128)(2,1)S(1)} custom-call(s32[1]{0:T(128)} %bitcast.me_ref, bf16[256,1024]{1,0:T(8,128)(2,1)S(1)} %slice.24.got, bf16[4,2,2,128,256]{4,3,2,1,0:T(8,128)(2,1)S(1)} %bitcast.29, bf16[4,2,2,128,256]{4,3,2,1,0:T(8,128)(2,1)} %bitcast.3.other), custom_call_target="tpu_custom_call" | custom-call | flops 536870912 | bytes 2621444 | tf_op jit(solution)/shard_map/pallas_call | solution.py:220
  129.9 0.0 copy-start.2
  129.9 1.0 copy-done.2
  130.9 0.0 reduce-scatter.2.cloned.1.call-update
  130.9 0.0 collective-permute-done.3.weights_other
  130.9 0.0 collective-permute-done.2.got_other
  130.9 2.8 %shard_map.158 = bf16[4,2,2,128,256]{4,3,2,1,0:T(8,128)(2,1)} custom-call(s32[1]{0:T(128)} %bitcast.me_ref, bf16[256,1024]{1,0:T(8,128)(2,1)S(1)} %slice.24.got, bf16[256,1024]{1,0:T(8,128)(2,1)} %collective-permute-done.2.got_other, bf16[8,2,136,256]{3,2,1,0:T(8,128)(2,1)S(1)} %bitcast.27, bf16[2,2,2,128,256]{4,3,2,1,0:T(8,128)(2,1)S(1)} %collective-permute-done.3.weights_other), custom_call_target="tpu_custom_call" | custom-call | flops 536870912 | bytes 2686980 | tf_op jit(solution)/shard_map/pallas_call | solution.py:220
  133.7 3.6 %all-to-all-start.3 = ((bf16[8,2,128,256]{3,2,1,0:T(8,128)(2,1)}), bf16[8,2,128,256]{3,2,1,0:T(8,128)(2,1)S(1)}, u32[]{:S(2)}, u32[]{:S(2)}) async-start(bf16[8,2,128,256]{3,2,1,0:T(8,128)(2,1)} %bitcast.11), calls=%async_computation.3 | async-start | bytes 2097152 | tf_op jit(solution)/shard_map/all_to_all | solution.py:306
  137.3 0.8 slice_bitcast_fusion.2
  138.1 0.7 copy.22
  138.9 28.0 %all-to-all-done.3 = bf16[8,2,128,256]{3,2,1,0:T(8,128)(2,1)S(1)} async-done(((bf16[8,2,128,256]{3,2,1,0:T(8,128)(2,1)}), bf16[8,2,128,256]{3,2,1,0:T(8,128)(2,1)S(1)}, u32[]{:S(2)}, u32[]{:S(2)}) %all-to-all-start.3) | async-done | bytes 1048608 | tf_op jit(solution)/shard_map/all_to_all | solution.py:306
  166.9 0.1 reduce_sum.12
  167.1 3.3 %collective-permute-start.4 = (bf16[2,128,256]{2,1,0:T(8,128)(2,1)S(1)}, bf16[2,128,256]{2,1,0:T(8,128)(2,1)S(1)}, u32[]{:S(2)}, u32[]{:S(2)}) collective-permute-start(bf16[2,128,256]{2,1,0:T(8,128)(2,1)S(1)} %reduce_sum.12), channel_id=1, source_target_pairs={{0,0},{1,1},{2,2},{3,3},{4,128},{5,129},{6,130},{7,131},{8,256},{9... | collective-permute-start | bytes 393224 | tf_op jit(solution)/shard_map/ppermute | solution.py:310
  170.4 0.0 reduce-scatter.2.cloned.1.call-done
  170.4 1.5 slice_bitcast_fusion
  171.9 0.7 copy.23
  172.6 9.3 %collective-permute-done.4 = bf16[2,128,256]{2,1,0:T(8,128)(2,1)S(1)} collective-permute-done((bf16[2,128,256]{2,1,0:T(8,128)(2,1)S(1)}, bf16[2,128,256]{2,1,0:T(8,128)(2,1)S(1)}, u32[]{:S(2)}, u32[]{:S(2)}) %collective-permute-start.4) | collective-permute-done | bytes 131104 | tf_op jit(solution)/shard_map/ppermute | solution.py:310
  181.9 0.7 slice_bitcast_fusion.3
Async XLA Ops:
  7.2 57.7 %all-gather.3.cloned.1.call-start = ((), (), s32[]{:S(2)}) async-start(), calls=%async_computation.6 | async-start | bytes 1253376 | tf_op jit(solution)/shard_map/all_gather | solution.py:242
  8.1 13.1 %collective-permute-start = (bf16[2,128,256]{2,1,0:T(8,128)(2,1)S(1)}, bf16[2,128,256]{2,1,0:T(8,128)(2,1)S(1)}, u32[]{:S(2)}, u32[]{:S(2)}) collective-permute-start(bf16[2,128,256]{2,1,0:T(8,128)(2,1)S(1)} %pad_maximum_fusion), channel_id=1, source_target_pairs={{0,0},{1,1},{2,2},{3,3},{4,128},{5,129},{6,130},{7,131},{8,256},{9... | collective-permute-start | bytes 393224 | tf_op jit(solution)/shard_map/ppermute | solution.py:243
  63.0 4.7 %collective-permute-start.1 = (bf16[8,2,128,256]{3,2,1,0:T(8,128)(2,1)S(1)}, bf16[8,2,128,256]{3,2,1,0:T(8,128)(2,1)}, u32[]{:S(2)}, u32[]{:S(2)}) collective-permute-start(bf16[8,2,128,256]{3,2,1,0:T(8,128)(2,1)S(1)} %all_to_all.20), channel_id=1, source_target_pairs={{0,1},{1,0},{2,3},{3,2},{4,5},{5,4},{6,7},{7,6},{8,9},{9,8},{10,11... | collective-permute-start | bytes 3145736 | tf_op jit(solution)/shard_map/ppermute | solution.py:246
  64.9 1.2 copy-start
  66.2 1.5 copy-start.1
  66.2 1.5 copy-start.3
  66.2 1.5 copy-start.4
  70.2 28.8 %copy-start.5 = (bf16[256,256]{1,0:T(8,128)(2,1)S(1)}, bf16[256,256]{1,0:T(8,128)(2,1)}, u32[]{:S(2)}) copy-start(bf16[256,256]{1,0:T(8,128)(2,1)} %constant.26.clone.second_back) | copy-start | bytes 393220
  70.2 28.8 %copy-start.6 = (bf16[256,256]{1,0:T(8,128)(2,1)S(1)}, bf16[256,256]{1,0:T(8,128)(2,1)}, u32[]{:S(2)}) copy-start(bf16[256,256]{1,0:T(8,128)(2,1)} %constant.25.clone.second) | copy-start | bytes 393220
  70.2 28.8 %copy-start.7 = (f32[64,128]{1,0:T(8,128)S(1)}, f32[64,128]{1,0:T(8,128)}, u32[]{:S(2)}) copy-start(f32[64,128]{1,0:T(8,128)} %constant.24.clone.twist_sin) | copy-start | bytes 98308
  70.2 28.8 %copy-start.8 = (f32[64,128]{1,0:T(8,128)S(1)}, f32[64,128]{1,0:T(8,128)}, u32[]{:S(2)}) copy-start(f32[64,128]{1,0:T(8,128)} %constant.23.clone.twist_cos) | copy-start | bytes 98308
  70.2 28.8 %copy-start.9 = (bf16[128,32]{1,0:T(8,128)(2,1)S(1)}, bf16[128,32]{1,0:T(8,128)(2,1)}, u32[]{:S(2)}) copy-start(bf16[128,32]{1,0:T(8,128)(2,1)} %constant.21.clone.first) | copy-start | bytes 24580
  70.2 28.8 %copy-start.10 = (bf16[32,128]{1,0:T(8,128)(2,1)S(1)}, bf16[32,128]{1,0:T(8,128)(2,1)}, u32[]{:S(2)}) copy-start(bf16[32,128]{1,0:T(8,128)(2,1)} %constant.22.clone.first_back) | copy-start | bytes 24580
  101.2 23.7 %all-to-all-start.2 = ((bf16[32,8,1152]{2,1,0:T(8,128)(2,1)}), bf16[32,8,1152]{2,1,0:T(8,128)(2,1)}, u32[]{:S(2)}, u32[]{:S(2)}) async-start(bf16[32,8,1152]{2,1,0:T(8,128)(2,1)} %shard_map.157), calls=%async_computation.2 | async-start | bytes 1179648 | tf_op jit(solution)/shard_map/all_to_all | solution.py:286
  107.0 63.3 %reduce-scatter.2.cloned.1.call-start = ((), (), s32[]{:S(2)}) async-start(), calls=%async_computation.5 | async-start | bytes 1179648 | tf_op jit(solution)/shard_map/reduce_scatter | solution.py:296
  107.1 23.8 %collective-permute-start.3 = (bf16[2,2,2,128,256]{4,3,2,1,0:T(8,128)(2,1)}, bf16[2,2,2,128,256]{4,3,2,1,0:T(8,128)(2,1)S(1)}, u32[]{:S(2)}, u32[]{:S(2)}) collective-permute-start(bf16[2,2,2,128,256]{4,3,2,1,0:T(8,128)(2,1)} %get-tuple-element.8), channel_id=1, source_target_pairs={{0,1},{1,0},{2,3},{3,2},{4,5},{5,4},{6,7},{7,6},{8,9},{9,8},{10,11... | collective-permute-start | bytes 1572872 | tf_op jit(solution)/shard_map/ppermute | solution.py:266
  126.0 4.9 %collective-permute-start.2 = (bf16[256,1024]{1,0:T(8,128)(2,1)S(1)}, bf16[256,1024]{1,0:T(8,128)(2,1)}, u32[]{:S(2)}, u32[]{:S(2)}) collective-permute-start(bf16[256,1024]{1,0:T(8,128)(2,1)S(1)} %slice.24.got), channel_id=1, source_target_pairs={{0,1},{1,0},{2,3},{3,2},{4,5},{5,4},{6,7},{7,6},{8,9},{9,8},{10,11... | collective-permute-start | bytes 1572872 | tf_op jit(solution)/shard_map/ppermute | solution.py:299
  129.9 1.0 copy-start.2
  133.7 33.2 %all-to-all-start.3 = ((bf16[8,2,128,256]{3,2,1,0:T(8,128)(2,1)}), bf16[8,2,128,256]{3,2,1,0:T(8,128)(2,1)S(1)}, u32[]{:S(2)}, u32[]{:S(2)}) async-start(bf16[8,2,128,256]{3,2,1,0:T(8,128)(2,1)} %bitcast.11), calls=%async_computation.3 | async-start | bytes 2097152 | tf_op jit(solution)/shard_map/all_to_all | solution.py:306
  167.1 14.8 %collective-permute-start.4 = (bf16[2,128,256]{2,1,0:T(8,128)(2,1)S(1)}, bf16[2,128,256]{2,1,0:T(8,128)(2,1)S(1)}, u32[]{:S(2)}, u32[]{:S(2)}) collective-permute-start(bf16[2,128,256]{2,1,0:T(8,128)(2,1)S(1)} %reduce_sum.12), channel_id=1, source_target_pairs={{0,0},{1,1},{2,2},{3,3},{4,128},{5,129},{6,130},{7,131},{8,256},{9... | collective-permute-start | bytes 393224 | tf_op jit(solution)/shard_map/ppermute | solution.py:310
Sparse Core Ops, SparseCore 0:
  16.8 45.0 all-gather.2
  131.0 32.4 reduce-scatter.1

commit v7 on v5

--- a/solution.py
+++ b/solution.py
@@ -191,19 +191,25 @@
                 out[4 * l + 2 * c + 1, which] = total[:, ROWS:]
 
 
-def output_kernel(me_ref, got, weights, keep, send):
-    me = me_ref[0]
+def output_terms(got, weights, which, l, c):
     half = NX * ROWS
-    for which in range(2):
-        start = which * half
-        rows = got[:, start : start + half].astype(f32).T.astype(bf16)
+    rows = got[:, which * half : (which + 1) * half].astype(f32).T.astype(bf16)
+    block = weight_block(weights, 1 - which, l, c)
+    total = lax.dot_general(rows, block, (((1,), (1,)), ((), ())), preferred_element_type=f32)
+    return total.reshape(NX, ROWS, 2 * ROWS)
+
+
+def send_kernel(me_ref, got, weights, send):
+    for which in range(2):
         for l in range(NL):
-            for held, c in ((keep, me), (send, 1 - me)):
-                block = weight_block(weights, 1 - which, l, c)
-                total = lax.dot_general(
-                    rows, block, (((1,), (1,)), ((), ())), preferred_element_type=f32
-                )
-                held[:, l, which] = total.astype(bf16).reshape(NX, ROWS, 2 * ROWS)
+            send[:, l, which] = output_terms(got, weights, which, l, 1 - me_ref[0]).astype(bf16)
+
+
+def keep_kernel(me_ref, got, weights, arrived, out):
+    for which in range(2):
+        for l in range(NL):
+            total = output_terms(got, weights, which, l, me_ref[0])
+            out[:, l, which] = (total + arrived[:, l, which].astype(f32)).astype(bf16)
 
 
 def call(kernel, inputs, out_shape, flops, scratch=(), first_smem=True):
@@ -287,11 +293,10 @@
     grad_input_weight, grad_output_weight = grads[0, 0].T, grads[0, 1]
 
     shape = jax.ShapeDtypeStruct(held, bf16)
-    keep, send = call(
-        output_kernel, (me, streams, weights), (shape, shape), 4 * half * 1024 * channels
-    )
+    flops = 2 * half * 1024 * channels
+    send = call(send_kernel, (me, streams, weights), shape, flops)
     arrived = lax.ppermute(send, "core", [(0, 1), (1, 0)])
-    parts = (keep.astype(f32) + arrived.astype(f32)).astype(bf16)
+    parts = call(keep_kernel, (me, streams, weights, arrived), shape, flops)
     parts = lax.all_to_all(
         parts.reshape(NH * NL, 2, tokens_here, features), Z, split_axis=0, concat_axis=0, tiled=True
     )

time: 187 us -> 189 us (1.011)
  Pallas kernels: 5.77 us -> 9.8 us
  other arithmetic: 5.07 us -> 2.54 us
    pallas_call x5 -> x6, Pallas kernels: 5.77 us -> 9.8 us  [call(): pl.pallas_call(kernel, out_shape=out_shape, in_specs=specs, out_specs=(VM...]
    convert_element_type x1 -> x0, other arithmetic: 2.52 us -> none  [on_device(): parts = (keep.astype(f32) + arrived.astype(f32)).astype(bf16)]
  transfers between devices with their start and end apart: 7 -> 7, of which waited for: 5 -> 4; matrix products, arithmetic and copies ran while one was open for 5% -> 3% of each run, Pallas kernels for 1% -> 3%
where the time goes in v7:
time: 189 us; the launch traced here: 188 us
  blocking collectives  93.9 us (50%)
  waiting for transfers between devices  43.7 us (23%)
  starting transfers between devices  16.8 us (9%)
  between operations  14.3 us (8%)
  Pallas kernels  9.8 us (5%)
  local copies, waits for them, and re-layouts  7.02 us (4%)
  other arithmetic  2.54 us (1%)
    all_to_all x1, blocking collectives, on_device(): own = lax.all_to_all(copies, Z, split_axis=0, concat_axis=0, tiled=True)  41.7 us
    all_to_all x1, waiting for transfers between devices, on_device(): lax.all_to_all(parts.reshape(NH * NL, 2, tokens_here, features), Z, split...  28.9 us
    all_to_all x1, blocking collectives, on_device(): lax.all_to_all(sent.reshape(BLOCKS, OWN, 2 * half + 2 * ROWS), CTX, split...  28.8 us
    all_to_all x1, blocking collectives, on_device(): got = lax.all_to_all(sent, CTX, split_axis=0, concat_axis=0, tiled=True)  23.4 us
    pallas_call x6, Pallas kernels, call(): pl.pallas_call(kernel, out_shape=out_shape, in_specs=specs, out_specs=(VM...  9.8 us
    ppermute x1, waiting for transfers between devices, on_device(): total = lax.ppermute(total, ALL, swap)  9.26 us
    ppermute x1, starting transfers between devices, on_device(): moved = lax.ppermute(jnp.stack([tokens, cotangent]), ALL, swap)  6.06 us
    unnamed x25, local copies, waits for them, and re-layouts  4.69 us
  transfers between devices with their start and end apart: 7, of which 4 were waited for; matrix products, arithmetic and copies ran while one was open for 3% of the time, Pallas kernels for 3%

profile of v7, /device:TPU:10, one launch (start us, length us, event | category | flops | bytes accessed | tf_op | source)
XLA Modules:
  0.0 188.0 jit_solution(15125957848404968860)
XLA Ops:
  7.2 0.0 all-gather.3.cloned.1.call-start
  7.2 0.9 pad_maximum_fusion
  8.1 6.1 %collective-permute-start = (bf16[2,128,256]{2,1,0:T(8,128)(2,1)S(1)}, bf16[2,128,256]{2,1,0:T(8,128)(2,1)S(1)}, u32[]{:S(2)}, u32[]{:S(2)}) collective-permute-start(bf16[2,128,256]{2,1,0:T(8,128)(2,1)S(1)} %pad_maximum_fusion), channel_id=1, source_target_pairs={{0,0},{1,1},{2,2},{3,3},{4,128},{5,129},{6,130},{7,131},{8,256},{9... | collective-permute-start | bytes 393224 | tf_op jit(solution)/shard_map/ppermute | solution.py:243
  14.2 0.9 copy.21
  15.1 1.5 fusion.2
  16.6 0.0 all-gather.3.cloned.1.call-update
  16.6 0.0 reduce-scatter.2.cloned.1.call-start
  16.7 4.5 %collective-permute-done = bf16[2,128,256]{2,1,0:T(8,128)(2,1)S(1)} collective-permute-done((bf16[2,128,256]{2,1,0:T(8,128)(2,1)S(1)}, bf16[2,128,256]{2,1,0:T(8,128)(2,1)S(1)}, u32[]{:S(2)}, u32[]{:S(2)}) %collective-permute-start) | collective-permute-done | bytes 131104 | tf_op jit(solution)/shard_map/ppermute | solution.py:243
  21.2 0.1 broadcast_in_dim.2
  21.3 41.7 %all_to_all.20 = bf16[8,2,128,256]{3,2,1,0:T(8,128)(2,1)S(1)} all-to-all(bf16[8,2,128,256]{3,2,1,0:T(8,128)(2,1)S(1)} %broadcast_in_dim.2), channel_id=1, replica_groups=mesh['x'=4,'y'=8,'zh'=4,'zl'=2,'core'=2] {'zh','zl'}, dimensions={0} | all-to-all | bytes 2097152 | tf_op jit(solution)/shard_map/all_to_all | solution.py:245
  63.0 1.9 %collective-permute-start.1 = (bf16[8,2,128,256]{3,2,1,0:T(8,128)(2,1)S(1)}, bf16[8,2,128,256]{3,2,1,0:T(8,128)(2,1)}, u32[]{:S(2)}, u32[]{:S(2)}) collective-permute-start(bf16[8,2,128,256]{3,2,1,0:T(8,128)(2,1)S(1)} %all_to_all.20), channel_id=1, source_target_pairs={{0,1},{1,0},{2,3},{3,2},{4,5},{5,4},{6,7},{7,6},{8,9},{9,8},{10,11... | collective-permute-start | bytes 3145736 | tf_op jit(solution)/shard_map/ppermute | solution.py:246
  64.9 0.0 all-gather.3.cloned.1.call-done
  64.9 0.0 copy-start
  64.9 1.2 copy-done
  66.2 0.0 copy-start.1
  66.2 0.0 copy-start.3
  66.2 0.0 copy-start.4
  66.2 0.4 shard_map.155.totals
  66.6 1.0 collective-permute-done.1
  67.6 0.0 copy-done.1
  67.6 0.0 copy-done.3
  67.6 0.0 copy-done.4
  67.6 1.8 shard_map.156
  69.4 0.0 copy-start.5
  69.5 0.0 copy-start.6
  69.5 0.0 copy-start.7
  69.5 0.0 copy-start.8
  69.5 0.0 copy-start.9
  69.5 0.0 copy-start.10
  69.5 28.8 %all_to_all.21.got = bf16[32,8,1280]{2,1,0:T(8,128)(2,1)S(1)} all-to-all(bf16[32,8,1280]{2,1,0:T(8,128)(2,1)S(1)} %bitcast.31), channel_id=1, replica_groups=mesh['x'=4,'y'=8,'zh'=4,'zl'=2,'core'=2] {'x','y'}, dimensions={0} | all-to-all | bytes 1310720 | tf_op jit(solution)/shard_map/all_to_all | solution.py:263
  98.3 0.0 copy-done.5
  98.3 0.0 copy-done.6
  98.3 0.0 copy-done.7
  98.3 0.0 copy-done.8
  98.3 0.0 copy-done.9
  98.3 0.0 copy-done.10
  98.3 1.3 shard_map.157
  99.6 23.4 %all_to_all.22 = bf16[32,8,1152]{2,1,0:T(8,128)(2,1)S(1)} all-to-all(bf16[32,8,1152]{2,1,0:T(8,128)(2,1)S(1)} %shard_map.157), channel_id=1, replica_groups=mesh['x'=4,'y'=8,'zh'=4,'zl'=2,'core'=2] {'x','y'}, dimensions={0} | all-to-all | bytes 1179648 | tf_op jit(solution)/shard_map/all_to_all | solution.py:282
  123.0 0.1 slice.24.got
  123.1 1.6 shard_map.158
  124.7 1.9 %collective-permute-start.2 = (bf16[4,2,2,128,256]{4,3,2,1,0:T(8,128)(2,1)}, bf16[4,2,2,128,256]{4,3,2,1,0:T(8,128)(2,1)}, u32[]{:S(2)}, u32[]{:S(2)}) collective-permute-start(bf16[4,2,2,128,256]{4,3,2,1,0:T(8,128)(2,1)} %shard_map.158), channel_id=1, source_target_pairs={{0,1},{1,0},{2,3},{3,2},{4,5},{5,4},{6,7},{7,6},{8,9},{9,8},{10,11... | collective-permute-start | bytes 3145736 | tf_op jit(solution)/shard_map/ppermute | solution.py:298
  126.6 1.9 %shard_map.160 = bf16[8,2,256,128]{3,2,1,0:T(8,128)(2,1)S(1)} custom-call(s32[1]{0:T(128)} %bitcast.me_ref, bf16[256,1024]{1,0:T(8,128)(2,1)S(1)} %slice.24.got, bf16[4,2,2,128,256]{4,3,2,1,0:T(8,128)(2,1)S(1)} %bitcast.30, bf16[4,2,2,128,256]{4,3,2,1,0:T(8,128)(2,1)} %bitcast.3.other), custom_call_target="tpu_custom_call" | custom-call | flops 536870912 | bytes 2621444 | tf_op jit(solution)/shard_map/pallas_call | solution.py:220
  128.5 0.0 copy-start.2
  128.5 1.0 copy-done.2
  129.5 0.0 reduce-scatter.2.cloned.1.call-update
  129.5 0.0 collective-permute-done.2.arrived
  129.5 2.8 %shard_map.159 = bf16[4,2,2,128,256]{4,3,2,1,0:T(8,128)(2,1)} custom-call(s32[1]{0:T(128)} %bitcast.me_ref, bf16[256,1024]{1,0:T(8,128)(2,1)S(1)} %slice.24.got, bf16[8,2,136,256]{3,2,1,0:T(8,128)(2,1)S(1)} %bitcast.28, bf16[4,2,2,128,256]{4,3,2,1,0:T(8,128)(2,1)} %collective-permute-done.2.arrived), custom_call_target="tpu_custom_call" | custom-call | flops 268435456 | bytes 2686980 | tf_op jit(solution)/shard_map/pallas_call | solution.py:220
  132.3 3.6 %all-to-all-start.3 = ((bf16[8,2,128,256]{3,2,1,0:T(8,128)(2,1)}), bf16[8,2,128,256]{3,2,1,0:T(8,128)(2,1)S(1)}, u32[]{:S(2)}, u32[]{:S(2)}) async-start(bf16[8,2,128,256]{3,2,1,0:T(8,128)(2,1)} %bitcast.11), calls=%async_computation.3 | async-start | bytes 2097152 | tf_op jit(solution)/shard_map/all_to_all | solution.py:300
  135.9 0.7 copy.22
  136.6 28.9 %all-to-all-done.3 = bf16[8,2,128,256]{3,2,1,0:T(8,128)(2,1)S(1)} async-done(((bf16[8,2,128,256]{3,2,1,0:T(8,128)(2,1)}), bf16[8,2,128,256]{3,2,1,0:T(8,128)(2,1)S(1)}, u32[]{:S(2)}, u32[]{:S(2)}) %all-to-all-start.3) | async-done | bytes 1048608 | tf_op jit(solution)/shard_map/all_to_all | solution.py:300
  165.5 0.1 reduce_sum.12
  165.7 3.3 %collective-permute-start.3 = (bf16[2,128,256]{2,1,0:T(8,128)(2,1)S(1)}, bf16[2,128,256]{2,1,0:T(8,128)(2,1)S(1)}, u32[]{:S(2)}, u32[]{:S(2)}) collective-permute-start(bf16[2,128,256]{2,1,0:T(8,128)(2,1)S(1)} %reduce_sum.12), channel_id=1, source_target_pairs={{0,0},{1,1},{2,2},{3,3},{4,128},{5,129},{6,130},{7,131},{8,256},{9... | collective-permute-start | bytes 393224 | tf_op jit(solution)/shard_map/ppermute | solution.py:304
  169.0 0.0 reduce-scatter.2.cloned.1.call-done
  169.0 1.5 slice_bitcast_fusion
  170.5 0.7 copy.23
  171.3 9.3 %collective-permute-done.3 = bf16[2,128,256]{2,1,0:T(8,128)(2,1)S(1)} collective-permute-done((bf16[2,128,256]{2,1,0:T(8,128)(2,1)S(1)}, bf16[2,128,256]{2,1,0:T(8,128)(2,1)S(1)}, u32[]{:S(2)}, u32[]{:S(2)}) %collective-permute-start.3) | collective-permute-done | bytes 131104 | tf_op jit(solution)/shard_map/ppermute | solution.py:304
  180.5 0.7 slice_bitcast_fusion.3
  (1 shorter events, 0.0 us)
Async XLA Ops:
  7.2 57.7 %all-gather.3.cloned.1.call-start = ((), (), s32[]{:S(2)}) async-start(), calls=%async_computation.6 | async-start | bytes 1253376 | tf_op jit(solution)/shard_map/all_gather | solution.py:242
  8.1 13.1 %collective-permute-start = (bf16[2,128,256]{2,1,0:T(8,128)(2,1)S(1)}, bf16[2,128,256]{2,1,0:T(8,128)(2,1)S(1)}, u32[]{:S(2)}, u32[]{:S(2)}) collective-permute-start(bf16[2,128,256]{2,1,0:T(8,128)(2,1)S(1)} %pad_maximum_fusion), channel_id=1, source_target_pairs={{0,0},{1,1},{2,2},{3,3},{4,128},{5,129},{6,130},{7,131},{8,256},{9... | collective-permute-start | bytes 393224 | tf_op jit(solution)/shard_map/ppermute | solution.py:243
  16.6 152.3 %reduce-scatter.2.cloned.1.call-start = ((), (), s32[]{:S(2)}) async-start(), calls=%async_computation.5 | async-start | bytes 1179648 | tf_op jit(solution)/shard_map/reduce_scatter | solution.py:292
  63.0 4.7 %collective-permute-start.1 = (bf16[8,2,128,256]{3,2,1,0:T(8,128)(2,1)S(1)}, bf16[8,2,128,256]{3,2,1,0:T(8,128)(2,1)}, u32[]{:S(2)}, u32[]{:S(2)}) collective-permute-start(bf16[8,2,128,256]{3,2,1,0:T(8,128)(2,1)S(1)} %all_to_all.20), channel_id=1, source_target_pairs={{0,1},{1,0},{2,3},{3,2},{4,5},{5,4},{6,7},{7,6},{8,9},{9,8},{10,11... | collective-permute-start | bytes 3145736 | tf_op jit(solution)/shard_map/ppermute | solution.py:246
  64.9 1.2 copy-start
  66.2 1.5 copy-start.1
  66.2 1.5 copy-start.3
  66.2 1.5 copy-start.4
  69.4 28.8 %copy-start.5 = (bf16[256,256]{1,0:T(8,128)(2,1)S(1)}, bf16[256,256]{1,0:T(8,128)(2,1)}, u32[]{:S(2)}) copy-start(bf16[256,256]{1,0:T(8,128)(2,1)} %constant.26.clone.second_back) | copy-start | bytes 393220
  69.5 28.8 %copy-start.6 = (bf16[256,256]{1,0:T(8,128)(2,1)S(1)}, bf16[256,256]{1,0:T(8,128)(2,1)}, u32[]{:S(2)}) copy-start(bf16[256,256]{1,0:T(8,128)(2,1)} %constant.25.clone.second) | copy-start | bytes 393220
  69.5 28.8 %copy-start.7 = (f32[64,128]{1,0:T(8,128)S(1)}, f32[64,128]{1,0:T(8,128)}, u32[]{:S(2)}) copy-start(f32[64,128]{1,0:T(8,128)} %constant.24.clone.twist_sin) | copy-start | bytes 98308
  69.5 28.8 %copy-start.8 = (f32[64,128]{1,0:T(8,128)S(1)}, f32[64,128]{1,0:T(8,128)}, u32[]{:S(2)}) copy-start(f32[64,128]{1,0:T(8,128)} %constant.23.clone.twist_cos) | copy-start | bytes 98308
  69.5 28.8 %copy-start.9 = (bf16[128,32]{1,0:T(8,128)(2,1)S(1)}, bf16[128,32]{1,0:T(8,128)(2,1)}, u32[]{:S(2)}) copy-start(bf16[128,32]{1,0:T(8,128)(2,1)} %constant.21.clone.first) | copy-start | bytes 24580
  69.5 28.8 %copy-start.10 = (bf16[32,128]{1,0:T(8,128)(2,1)S(1)}, bf16[32,128]{1,0:T(8,128)(2,1)}, u32[]{:S(2)}) copy-start(bf16[32,128]{1,0:T(8,128)(2,1)} %constant.22.clone.first_back) | copy-start | bytes 24580
  124.7 4.9 %collective-permute-start.2 = (bf16[4,2,2,128,256]{4,3,2,1,0:T(8,128)(2,1)}, bf16[4,2,2,128,256]{4,3,2,1,0:T(8,128)(2,1)}, u32[]{:S(2)}, u32[]{:S(2)}) collective-permute-start(bf16[4,2,2,128,256]{4,3,2,1,0:T(8,128)(2,1)} %shard_map.158), channel_id=1, source_target_pairs={{0,1},{1,0},{2,3},{3,2},{4,5},{5,4},{6,7},{7,6},{8,9},{9,8},{10,11... | collective-permute-start | bytes 3145736 | tf_op jit(solution)/shard_map/ppermute | solution.py:298
  128.5 1.0 copy-start.2
  132.3 33.2 %all-to-all-start.3 = ((bf16[8,2,128,256]{3,2,1,0:T(8,128)(2,1)}), bf16[8,2,128,256]{3,2,1,0:T(8,128)(2,1)S(1)}, u32[]{:S(2)}, u32[]{:S(2)}) async-start(bf16[8,2,128,256]{3,2,1,0:T(8,128)(2,1)} %bitcast.11), calls=%async_computation.3 | async-start | bytes 2097152 | tf_op jit(solution)/shard_map/all_to_all | solution.py:300
  165.7 14.8 %collective-permute-start.3 = (bf16[2,128,256]{2,1,0:T(8,128)(2,1)S(1)}, bf16[2,128,256]{2,1,0:T(8,128)(2,1)S(1)}, u32[]{:S(2)}, u32[]{:S(2)}) collective-permute-start(bf16[2,128,256]{2,1,0:T(8,128)(2,1)S(1)} %reduce_sum.12), channel_id=1, source_target_pairs={{0,0},{1,1},{2,2},{3,3},{4,128},{5,129},{6,130},{7,131},{8,256},{9... | collective-permute-start | bytes 393224 | tf_op jit(solution)/shard_map/ppermute | solution.py:304
Sparse Core Ops, SparseCore 0:
  16.8 45.0 all-gather.2
  129.7 32.4 reduce-scatter.1
